TPU v7x, 512 devices: a whole 4x8x8 slice. The times are simulated.
512 devices in a mesh: layer: 8 (over z), row: 8 (over x, core), col: 8 (over y).
Axes of the slice: x: 4, y: 8, z: 8, core: 2. Of those that a mesh axis runs over, the one named last changes fastest.
Arguments:
- c_states: float32 [8, 64, 64, 1024], P('layer', None, 'row', 'col'), may hold values from -6 to 6
- c_adjoints: float32 [8, 64, 64, 1024], P('layer', None, 'row', 'col'), may hold values from -6 to 6
- weights: bfloat16 [32, 64, 576], P('layer'), may hold values from -0.25 to 0.25
Outputs:
- new_states: float32 [8, 64, 64, 1024], P('layer', None, 'row', 'col')
- new_adjoints: float32 [8, 64, 64, 1024], P('layer', None, 'row', 'col')
- weight_grads: float32 [32, 64, 576], P('layer')
All inputs are finite; a program needn't handle non-finite values.
Results may differ from a plain program's by a relative error of at most 0.006.
Values may be sent and summed in bfloat16 or wider, within the bound.
A program may use at most 64 MiB of HBM per device.

v0:
```python
import jax
import jax.numpy as jnp
from jax import lax
from jax.sharding import PartitionSpec as P

step_size = 0.2


def with_halo(cells, sides, width):
    for axis, dim in sides:
        count = lax.axis_size(axis)
        ends = count - 1
        head = lax.slice_in_dim(cells, 0, width, axis=dim)
        tail = lax.slice_in_dim(cells, cells.shape[dim] - width, cells.shape[dim], axis=dim)
        cells = jnp.concatenate(
            [
                lax.ppermute(tail, axis, [(i, (i + 1) % count) for i in range(ends)]),
                cells,
                lax.ppermute(head, axis, [((i + 1) % count, i) for i in range(ends)]),
            ],
            axis=dim,
        )
    return cells


def from_behind(array, axis, by):
    devices = lax.axis_size(axis)
    pairs = [(i, i + by) for i in range(devices) if 0 <= i + by < devices]
    return lax.ppermute(array, axis, pairs)


def tile_patches(padded, tile_rows, tile_cols):
    shifted = [
        padded[:, row_off : row_off + tile_rows, col_off : col_off + tile_cols].reshape(
            padded.shape[0], tile_rows * tile_cols
        )
        for row_off in range(3)
        for col_off in range(3)
    ]
    return jnp.concatenate(shifted, 0)


def exact_dot(left_mat, right_mat):
    return jnp.dot(
        left_mat, right_mat, precision=lax.Precision.HIGHEST, preferred_element_type=jnp.float32
    )


def flipped(weight_mat):
    channels = weight_mat.shape[0]
    return jnp.transpose(weight_mat.reshape(channels, 9, channels)[:, ::-1, :], (2, 1, 0)).reshape(
        channels, 9 * channels
    )


def local(c_states, c_adjoints, weights):
    group_index = lax.axis_index("layer")
    group_count = lax.axis_size("layer")
    channels, tile_rows, tile_cols = c_states.shape[1:]
    pixels = tile_rows * tile_cols
    depth = weights.shape[0]
    initial_flat = c_states[0].reshape(channels, pixels)
    guess_flat = c_adjoints[0].reshape(channels, pixels)

    def advance(state, weight_mat):
        active = state.astype(jnp.bfloat16).reshape(channels, tile_rows, tile_cols)
        padded = with_halo(active, (("row", 1), ("col", 2)), 1)
        preact = jnp.dot(
            weight_mat,
            tile_patches(padded, tile_rows, tile_cols),
            preferred_element_type=jnp.float32,
        )
        return (state + step_size * jnp.tanh(preact), padded, preact)

    state = initial_flat
    for layer_pos in range(depth):
        state, _, _ = advance(state, weights[layer_pos])
    group_end = state
    summed = jnp.sum(weights[0].astype(jnp.float32).reshape(channels, 9, channels), axis=1)
    coarse_map = jnp.eye(channels, dtype=jnp.float32) + step_size * summed
    is_first = group_index == 0
    is_last = group_index == group_count - 1
    zero_map = jnp.zeros_like(coarse_map)
    blank = jnp.zeros((channels, pixels), jnp.float32)
    fwd_map = jnp.where(is_first, zero_map, coarse_map)
    fwd_offset = jnp.where(is_first, group_end, group_end - exact_dot(coarse_map, initial_flat))

    def state_turn(turn_number, carried):
        return from_behind(exact_dot(fwd_map, carried) + fwd_offset, "layer", 1)

    arrived = lax.fori_loop(0, group_count - 1, state_turn, blank)
    corrected = jnp.where(is_first, initial_flat, arrived)
    state = corrected
    trail = []
    for layer_pos in range(depth):
        state, padded, preact = advance(state, weights[layer_pos])
        trail.append((padded, preact))
    adjoint = guess_flat
    grad_list = [None] * depth
    for layer_pos in reversed(range(depth)):
        padded, preact = trail[layer_pos]
        slope = jnp.tanh(preact)
        source = (adjoint * step_size * (1.0 - slope * slope)).astype(jnp.bfloat16)
        source_pad = with_halo(
            source.reshape(channels, tile_rows, tile_cols), (("row", 1), ("col", 2)), 1
        )
        grad_list[layer_pos] = lax.dot_general(
            source,
            tile_patches(padded, tile_rows, tile_cols),
            (((1,), (1,)), ((), ())),
            preferred_element_type=jnp.float32,
        )
        back = jnp.dot(
            flipped(weights[layer_pos]),
            tile_patches(source_pad, tile_rows, tile_cols),
            preferred_element_type=jnp.float32,
        )
        adjoint = adjoint + back
    weight_grads = lax.psum(jnp.stack(grad_list, 0), ("row", "col"))
    transposed = coarse_map.T
    back_map = jnp.where(is_last, zero_map, transposed)
    back_offset = jnp.where(is_last, adjoint, adjoint - exact_dot(transposed, guess_flat))

    def adjoint_turn(turn_number, carried):
        return from_behind(exact_dot(back_map, carried) + back_offset, "layer", -1)

    returned = lax.fori_loop(0, group_count - 1, adjoint_turn, blank)
    new_adjoint = jnp.where(is_last, guess_flat, returned)
    out_shape = (1, channels, tile_rows, tile_cols)
    return (corrected.reshape(out_shape), new_adjoint.reshape(out_shape), weight_grads)


def solution(mesh):
    placed = (
        P("layer", None, "row", "col"),
        P("layer", None, "row", "col"),
        P("layer", None, None),
    )
    return jax.shard_map(
        local,
        mesh=mesh,
        in_specs=placed,
        out_specs=(
            P("layer", None, "row", "col"),
            P("layer", None, "row", "col"),
            P("layer", None, None),
        ),
        check_vma=False,
    )
```

profile of v0, /device:TPU:1, one launch (start us, length us, event | category | flops | bytes accessed | tf_op | source)
XLA Modules:
  0.0 560.1 jit_solution(8448254401400745606)
XLA Ops:
  8.2 4.5 collective-permute-start.2
  12.8 5.6 collective-permute-start.3
  22.8 4.6 collective-permute-done.4
  27.9 3.7 collective-permute-done.5
  38.6 3.3 collective-permute-done.7
  42.2 3.2 collective-permute-start.8
  46.7 3.1 collective-permute-done.8
  50.3 3.6 collective-permute-done.9
  55.3 3.9 collective-permute-start.10
  61.1 3.3 collective-permute-done.11
  64.7 5.2 collective-permute-start.12
  74.9 4.8 collective-permute-done.13
  81.0 4.5 collective-permute-start.14
  87.5 3.2 collective-permute-done.15
  91.1 3.8 collective-permute-start.16
  96.3 3.0 collective-permute-done.16
  99.8 3.7 collective-permute-done.17
  105.2 64.2 %while.20 = (s32[]{:T(128)}, f32[64,1024]{1,0:T(8,128)S(1)}, f32[64,64]{1,0:T(8,128)S(1)}, f32[64,1024]{1,0:T(8,128)S(1)}, s32[]{:T(128)}) while((s32[]{:T(128)}, f32[64,1024]{1,0:T(8,128)S(1)}, f32[64,64]{1,0:T(8,128)S(1)}, f32[64,1024]{1,0:T(8,128)S(1)}, s32[]{:T(128)}) %tuple.143), condition=%wide.region_2.3_spmd, body=%wide.region_1.2_spmd.sunk | while | flops 50397184 | bytes 1851493 | solution.py:91
  105.6 4.0 collective-permute-start
  109.6 5.8 %collective-permute-done = f32[64,1024]{1,0:T(8,128)S(1)} collective-permute-done((f32[64,1024]{1,0:T(8,128)S(1)}, f32[64,1024]{1,0:T(8,128)S(1)}, u32[]{:S(2)}, u32[]{:S(2)}) %collective-permute-start) | collective-permute-done | bytes 262176 | tf_op jit(solution)/shard_map/while/body/eval_jaxpr/ppermute | solution.py:29
  115.8 4.0 collective-permute-start
  119.8 5.5 collective-permute-done
  125.7 4.1 collective-permute-start
  129.8 4.5 collective-permute-done
  134.7 5.4 collective-permute-start
  140.1 3.8 collective-permute-done
  144.3 4.1 collective-permute-start
  148.4 3.3 collective-permute-done
  152.0 5.1 collective-permute-start
  157.1 3.3 collective-permute-done
  160.8 5.3 collective-permute-start
  166.1 3.3 collective-permute-done
  169.5 6.1 %collective-permute-start.18 = (bf16[64,1,128]{2,1,0:T(2,128)(2,1)S(1)}, bf16[64,1,128]{2,1,0:T(2,128)(2,1)S(1)}, u32[]{:S(2)}, u32[]{:S(2)}) collective-permute-start(bf16[64,1,128]{2,1,0:T(2,128)(2,1)S(1)} %get-tuple-element.215), channel_id=1, source_target_pairs={{0,8},{8,16},{16,24},{24,32},{32,40},{40,48},{48,56},{1,9},{9,17},... | collective-permute-start | bytes 49160 | tf_op jit(solution)/shard_map/ppermute | solution.py:17
  175.6 2.9 collective-permute-start.19
  185.0 3.7 collective-permute-done.20
  189.2 3.6 collective-permute-done.21
  198.6 3.3 collective-permute-done.23
  202.2 3.9 collective-permute-start.24
  207.4 3.1 collective-permute-done.24
  211.0 4.6 collective-permute-done.25
  217.8 4.2 collective-permute-start.26
  223.9 3.3 collective-permute-done.27
  228.2 3.5 collective-permute-start.28
  237.4 3.0 collective-permute-done.29
  247.1 3.1 collective-permute-done.31
  251.3 3.7 collective-permute-start.32
  260.7 3.8 collective-permute-done.33
  277.7 3.4 collective-permute-start.36
  288.2 6.2 %collective-permute-done.37 = bf16[64,10,1]{2,1,0:T(8,128)(2,1)S(1)} collective-permute-done((bf16[64,10,1]{2,1,0:T(8,128)(2,1)}, bf16[64,10,1]{2,1,0:T(8,128)(2,1)S(1)}, u32[]{:S(2)}, u32[]{:S(2)}) %collective-permute-start.37) | collective-permute-done | bytes 1312 | tf_op jit(solution)/shard_map/ppermute | solution.py:19
  313.3 4.2 collective-permute-done.40
  318.0 4.1 collective-permute-done.41
  331.8 3.1 collective-permute-start.44
  336.7 3.1 collective-permute-done.44
  340.3 4.1 collective-permute-done.45
  362.3 4.5 collective-permute-done.49
  369.2 71.1 %while.21 = (s32[]{:T(128)}, f32[64,1024]{1,0:T(8,128)S(1)}, f32[64,64]{1,0:T(8,128)S(1)}, f32[64,1024]{1,0:T(8,128)S(1)}, s32[]{:T(128)}) while((s32[]{:T(128)}, f32[64,1024]{1,0:T(8,128)S(1)}, f32[64,64]{1,0:T(8,128)S(1)}, f32[64,1024]{1,0:T(8,128)S(1)}, s32[]{:T(128)}) %tuple.146), condition=%wide.region_4.5_spmd, body=%wide.region_3.4_spmd.sunk | while | flops 50397184 | bytes 1851493 | solution.py:127
  370.9 10.6 %collective-permute-done.1 = f32[64,1024]{1,0:T(8,128)S(1)} collective-permute-done((f32[64,1024]{1,0:T(8,128)S(1)}, f32[64,1024]{1,0:T(8,128)S(1)}, u32[]{:S(2)}, u32[]{:S(2)}) %collective-permute-start.1) | collective-permute-done | bytes 262176 | tf_op jit(solution)/shard_map/while/body/eval_jaxpr/ppermute | solution.py:29
  383.2 10.7 %collective-permute-done.1 = f32[64,1024]{1,0:T(8,128)S(1)} collective-permute-done((f32[64,1024]{1,0:T(8,128)S(1)}, f32[64,1024]{1,0:T(8,128)S(1)}, u32[]{:S(2)}, u32[]{:S(2)}) %collective-permute-start.1) | collective-permute-done | bytes 262176 | tf_op jit(solution)/shard_map/while/body/eval_jaxpr/ppermute | solution.py:29
  395.6 10.1 %collective-permute-done.1 = f32[64,1024]{1,0:T(8,128)S(1)} collective-permute-done((f32[64,1024]{1,0:T(8,128)S(1)}, f32[64,1024]{1,0:T(8,128)S(1)}, u32[]{:S(2)}, u32[]{:S(2)}) %collective-permute-start.1) | collective-permute-done | bytes 262176 | tf_op jit(solution)/shard_map/while/body/eval_jaxpr/ppermute | solution.py:29
  407.3 9.0 %collective-permute-done.1 = f32[64,1024]{1,0:T(8,128)S(1)} collective-permute-done((f32[64,1024]{1,0:T(8,128)S(1)}, f32[64,1024]{1,0:T(8,128)S(1)}, u32[]{:S(2)}, u32[]{:S(2)}) %collective-permute-start.1) | collective-permute-done | bytes 262176 | tf_op jit(solution)/shard_map/while/body/eval_jaxpr/ppermute | solution.py:29
  418.0 6.4 %collective-permute-done.1 = f32[64,1024]{1,0:T(8,128)S(1)} collective-permute-done((f32[64,1024]{1,0:T(8,128)S(1)}, f32[64,1024]{1,0:T(8,128)S(1)}, u32[]{:S(2)}, u32[]{:S(2)}) %collective-permute-start.1) | collective-permute-done | bytes 262176 | tf_op jit(solution)/shard_map/while/body/eval_jaxpr/ppermute | solution.py:29
  426.1 5.8 %collective-permute-done.1 = f32[64,1024]{1,0:T(8,128)S(1)} collective-permute-done((f32[64,1024]{1,0:T(8,128)S(1)}, f32[64,1024]{1,0:T(8,128)S(1)}, u32[]{:S(2)}, u32[]{:S(2)}) %collective-permute-start.1) | collective-permute-done | bytes 262176 | tf_op jit(solution)/shard_map/while/body/eval_jaxpr/ppermute | solution.py:29
  433.5 6.8 %collective-permute-done.1 = f32[64,1024]{1,0:T(8,128)S(1)} collective-permute-done((f32[64,1024]{1,0:T(8,128)S(1)}, f32[64,1024]{1,0:T(8,128)S(1)}, u32[]{:S(2)}, u32[]{:S(2)}) %collective-permute-start.1) | collective-permute-done | bytes 262176 | tf_op jit(solution)/shard_map/while/body/eval_jaxpr/ppermute | solution.py:29
  441.1 110.2 %all-reduce.2.cloned.1.call-done = f32[4,64,576]{2,1,0:T(8,128)} async-done(((f32[4,64,576]{2,1,0:T(8,128)}), f32[4,64,576]{2,1,0:T(8,128)}) %all-reduce.2.cloned.1.call-update) | async-done | bytes 589840 | tf_op jit(solution)/shard_map/psum | solution.py:119
  (360 shorter events, 157.1 us)
Async XLA Ops:
  7.2 544.2 %all-reduce.2.cloned.1.call-start = ((), (), s32[]{:S(2)}) async-start(), calls=%async_computation | async-start | bytes 1310720 | tf_op jit(solution)/shard_map/psum | solution.py:119
  8.2 10.1 %collective-permute-start.2 = (bf16[64,1,128]{2,1,0:T(2,128)(2,1)S(1)}, bf16[64,1,128]{2,1,0:T(2,128)(2,1)S(1)}, u32[]{:S(2)}, u32[]{:S(2)}) collective-permute-start(bf16[64,1,128]{2,1,0:T(2,128)(2,1)S(1)} %get-tuple-element.223), channel_id=1, source_target_pairs={{0,8},{8,16},{16,24},{24,32},{32,40},{40,48},{48,56},{1,9},{9,17},... | collective-permute-start | bytes 49160 | tf_op jit(solution)/shard_map/ppermute | solution.py:17
  12.8 6.4 %collective-permute-start.3 = (bf16[64,1,128]{2,1,0:T(2,128)(2,1)S(1)}, bf16[64,1,128]{2,1,0:T(2,128)(2,1)S(1)}, u32[]{:S(2)}, u32[]{:S(2)}) collective-permute-start(bf16[64,1,128]{2,1,0:T(2,128)(2,1)S(1)} %get-tuple-element.224), channel_id=1, source_target_pairs={{8,0},{16,8},{24,16},{32,24},{40,32},{48,40},{56,48},{9,1},{17,9},... | collective-permute-start | bytes 49160 | tf_op jit(solution)/shard_map/ppermute | solution.py:19
  19.5 7.9 %collective-permute-start.4 = (bf16[64,10,1]{2,1,0:T(8,128)(2,1)S(1)}, bf16[64,10,1]{2,1,0:T(8,128)(2,1)S(1)}, u32[]{:S(2)}, u32[]{:S(2)}) collective-permute-start(bf16[64,10,1]{2,1,0:T(8,128)(2,1)S(1)} %get-tuple-element.176), channel_id=1, source_target_pairs={{0,1},{1,2},{2,3},{3,4},{4,5},{5,6},{6,7},{8,9},{9,10},{10,11},{11... | collective-permute-start | bytes 3848 | tf_op jit(solution)/shard_map/ppermute | solution.py:17
  21.5 10.1 %collective-permute-start.5 = (bf16[64,10,1]{2,1,0:T(8,128)(2,1)S(1)}, bf16[64,10,1]{2,1,0:T(8,128)(2,1)S(1)}, u32[]{:S(2)}, u32[]{:S(2)}) collective-permute-start(bf16[64,10,1]{2,1,0:T(8,128)(2,1)S(1)} %get-tuple-element.175), channel_id=1, source_target_pairs={{1,0},{2,1},{3,2},{4,3},{5,4},{6,5},{7,6},{9,8},{10,9},{11,10},{12... | collective-permute-start | bytes 3848 | tf_op jit(solution)/shard_map/ppermute | solution.py:19
  33.8 4.8 collective-permute-start.6
  36.7 5.2 collective-permute-start.7
  42.2 7.6 %collective-permute-start.8 = (bf16[64,10,1]{2,1,0:T(8,128)(2,1)S(1)}, bf16[64,10,1]{2,1,0:T(8,128)(2,1)S(1)}, u32[]{:S(2)}, u32[]{:S(2)}) collective-permute-start(bf16[64,10,1]{2,1,0:T(8,128)(2,1)S(1)} %get-tuple-element.174), channel_id=1, source_target_pairs={{0,1},{1,2},{2,3},{3,4},{4,5},{5,6},{6,7},{8,9},{9,10},{10,11},{11... | collective-permute-start | bytes 3848 | tf_op jit(solution)/shard_map/ppermute | solution.py:17
  45.4 8.5 %collective-permute-start.9 = (bf16[64,10,1]{2,1,0:T(8,128)(2,1)S(1)}, bf16[64,10,1]{2,1,0:T(8,128)(2,1)S(1)}, u32[]{:S(2)}, u32[]{:S(2)}) collective-permute-start(bf16[64,10,1]{2,1,0:T(8,128)(2,1)S(1)} %get-tuple-element.173), channel_id=1, source_target_pairs={{1,0},{2,1},{3,2},{4,3},{5,4},{6,5},{7,6},{9,8},{10,9},{11,10},{12... | collective-permute-start | bytes 3848 | tf_op jit(solution)/shard_map/ppermute | solution.py:19
  55.3 5.8 %collective-permute-start.10 = (bf16[64,1,128]{2,1,0:T(2,128)(2,1)S(1)}, bf16[64,1,128]{2,1,0:T(2,128)(2,1)S(1)}, u32[]{:S(2)}, u32[]{:S(2)}) collective-permute-start(bf16[64,1,128]{2,1,0:T(2,128)(2,1)S(1)} %get-tuple-element.219), channel_id=1, source_target_pairs={{0,8},{8,16},{16,24},{24,32},{32,40},{40,48},{48,56},{1,9},{9,17},... | collective-permute-start | bytes 49160 | tf_op jit(solution)/shard_map/ppermute | solution.py:17
  59.2 5.2 collective-permute-start.11
  64.7 9.7 %collective-permute-start.12 = (bf16[64,10,1]{2,1,0:T(8,128)(2,1)S(1)}, bf16[64,10,1]{2,1,0:T(8,128)(2,1)S(1)}, u32[]{:S(2)}, u32[]{:S(2)}) collective-permute-start(bf16[64,10,1]{2,1,0:T(8,128)(2,1)S(1)} %get-tuple-element.172), channel_id=1, source_target_pairs={{0,1},{1,2},{2,3},{3,4},{4,5},{5,6},{6,7},{8,9},{9,10},{10,11},{11... | collective-permute-start | bytes 3848 | tf_op jit(solution)/shard_map/ppermute | solution.py:17
  70.8 8.9 %collective-permute-start.13 = (bf16[64,10,1]{2,1,0:T(8,128)(2,1)S(1)}, bf16[64,10,1]{2,1,0:T(8,128)(2,1)S(1)}, u32[]{:S(2)}, u32[]{:S(2)}) collective-permute-start(bf16[64,10,1]{2,1,0:T(8,128)(2,1)S(1)} %get-tuple-element.171), channel_id=1, source_target_pairs={{1,0},{2,1},{3,2},{4,3},{5,4},{6,5},{7,6},{9,8},{10,9},{11,10},{12... | collective-permute-start | bytes 3848 | tf_op jit(solution)/shard_map/ppermute | solution.py:19
  81.0 6.5 %collective-permute-start.14 = (bf16[64,1,128]{2,1,0:T(2,128)(2,1)S(1)}, bf16[64,1,128]{2,1,0:T(2,128)(2,1)S(1)}, u32[]{:S(2)}, u32[]{:S(2)}) collective-permute-start(bf16[64,1,128]{2,1,0:T(2,128)(2,1)S(1)} %get-tuple-element.217), channel_id=1, source_target_pairs={{0,8},{8,16},{16,24},{24,32},{32,40},{40,48},{48,56},{1,9},{9,17},... | collective-permute-start | bytes 49160 | tf_op jit(solution)/shard_map/ppermute | solution.py:17
  85.5 5.2 collective-permute-start.15
  91.1 8.2 %collective-permute-start.16 = (bf16[64,10,1]{2,1,0:T(8,128)(2,1)S(1)}, bf16[64,10,1]{2,1,0:T(8,128)(2,1)S(1)}, u32[]{:S(2)}, u32[]{:S(2)}) collective-permute-start(bf16[64,10,1]{2,1,0:T(8,128)(2,1)S(1)} %get-tuple-element.170), channel_id=1, source_target_pairs={{0,1},{1,2},{2,3},{3,4},{4,5},{5,6},{6,7},{8,9},{9,10},{10,11},{11... | collective-permute-start | bytes 3848 | tf_op jit(solution)/shard_map/ppermute | solution.py:17
  95.0 8.5 %collective-permute-start.17 = (bf16[64,10,1]{2,1,0:T(8,128)(2,1)S(1)}, bf16[64,10,1]{2,1,0:T(8,128)(2,1)S(1)}, u32[]{:S(2)}, u32[]{:S(2)}) collective-permute-start(bf16[64,10,1]{2,1,0:T(8,128)(2,1)S(1)} %get-tuple-element.169), channel_id=1, source_target_pairs={{1,0},{2,1},{3,2},{4,3},{5,4},{6,5},{7,6},{9,8},{10,9},{11,10},{12... | collective-permute-start | bytes 3848 | tf_op jit(solution)/shard_map/ppermute | solution.py:19
  105.6 9.8 %collective-permute-start = (f32[64,1024]{1,0:T(8,128)S(1)}, f32[64,1024]{1,0:T(8,128)S(1)}, u32[]{:S(2)}, u32[]{:S(2)}) collective-permute-start(f32[64,1024]{1,0:T(8,128)S(1)} %convolution_add_fusion.4), channel_id=1, source_target_pairs={{0,64},{64,128},{128,192},{192,256},{256,320},{320,384},{384,448},... | collective-permute-start | bytes 786440 | tf_op jit(solution)/shard_map/while/body/eval_jaxpr/ppermute | solution.py:29
  115.8 9.5 %collective-permute-start = (f32[64,1024]{1,0:T(8,128)S(1)}, f32[64,1024]{1,0:T(8,128)S(1)}, u32[]{:S(2)}, u32[]{:S(2)}) collective-permute-start(f32[64,1024]{1,0:T(8,128)S(1)} %convolution_add_fusion.4), channel_id=1, source_target_pairs={{0,64},{64,128},{128,192},{192,256},{256,320},{320,384},{384,448},... | collective-permute-start | bytes 786440 | tf_op jit(solution)/shard_map/while/body/eval_jaxpr/ppermute | solution.py:29
  125.7 8.7 %collective-permute-start = (f32[64,1024]{1,0:T(8,128)S(1)}, f32[64,1024]{1,0:T(8,128)S(1)}, u32[]{:S(2)}, u32[]{:S(2)}) collective-permute-start(f32[64,1024]{1,0:T(8,128)S(1)} %convolution_add_fusion.4), channel_id=1, source_target_pairs={{0,64},{64,128},{128,192},{192,256},{256,320},{320,384},{384,448},... | collective-permute-start | bytes 786440 | tf_op jit(solution)/shard_map/while/body/eval_jaxpr/ppermute | solution.py:29
  134.7 9.2 %collective-permute-start = (f32[64,1024]{1,0:T(8,128)S(1)}, f32[64,1024]{1,0:T(8,128)S(1)}, u32[]{:S(2)}, u32[]{:S(2)}) collective-permute-start(f32[64,1024]{1,0:T(8,128)S(1)} %convolution_add_fusion.4), channel_id=1, source_target_pairs={{0,64},{64,128},{128,192},{192,256},{256,320},{320,384},{384,448},... | collective-permute-start | bytes 786440 | tf_op jit(solution)/shard_map/while/body/eval_jaxpr/ppermute | solution.py:29
  144.3 7.4 %collective-permute-start = (f32[64,1024]{1,0:T(8,128)S(1)}, f32[64,1024]{1,0:T(8,128)S(1)}, u32[]{:S(2)}, u32[]{:S(2)}) collective-permute-start(f32[64,1024]{1,0:T(8,128)S(1)} %convolution_add_fusion.4), channel_id=1, source_target_pairs={{0,64},{64,128},{128,192},{192,256},{256,320},{320,384},{384,448},... | collective-permute-start | bytes 786440 | tf_op jit(solution)/shard_map/while/body/eval_jaxpr/ppermute | solution.py:29
  152.0 8.3 %collective-permute-start = (f32[64,1024]{1,0:T(8,128)S(1)}, f32[64,1024]{1,0:T(8,128)S(1)}, u32[]{:S(2)}, u32[]{:S(2)}) collective-permute-start(f32[64,1024]{1,0:T(8,128)S(1)} %convolution_add_fusion.4), channel_id=1, source_target_pairs={{0,64},{64,128},{128,192},{192,256},{256,320},{320,384},{384,448},... | collective-permute-start | bytes 786440 | tf_op jit(solution)/shard_map/while/body/eval_jaxpr/ppermute | solution.py:29
  160.8 8.6 %collective-permute-start = (f32[64,1024]{1,0:T(8,128)S(1)}, f32[64,1024]{1,0:T(8,128)S(1)}, u32[]{:S(2)}, u32[]{:S(2)}) collective-permute-start(f32[64,1024]{1,0:T(8,128)S(1)} %convolution_add_fusion.4), channel_id=1, source_target_pairs={{0,64},{64,128},{128,192},{192,256},{256,320},{320,384},{384,448},... | collective-permute-start | bytes 786440 | tf_op jit(solution)/shard_map/while/body/eval_jaxpr/ppermute | solution.py:29
  169.5 9.0 %collective-permute-start.18 = (bf16[64,1,128]{2,1,0:T(2,128)(2,1)S(1)}, bf16[64,1,128]{2,1,0:T(2,128)(2,1)S(1)}, u32[]{:S(2)}, u32[]{:S(2)}) collective-permute-start(bf16[64,1,128]{2,1,0:T(2,128)(2,1)S(1)} %get-tuple-element.215), channel_id=1, source_target_pairs={{0,8},{8,16},{16,24},{24,32},{32,40},{40,48},{48,56},{1,9},{9,17},... | collective-permute-start | bytes 49160 | tf_op jit(solution)/shard_map/ppermute | solution.py:17
  175.6 5.2 collective-permute-start.19
  181.1 7.6 %collective-permute-start.20 = (bf16[64,10,1]{2,1,0:T(8,128)(2,1)S(1)}, bf16[64,10,1]{2,1,0:T(8,128)(2,1)S(1)}, u32[]{:S(2)}, u32[]{:S(2)}) collective-permute-start(bf16[64,10,1]{2,1,0:T(8,128)(2,1)S(1)} %get-tuple-element.168), channel_id=1, source_target_pairs={{0,1},{1,2},{2,3},{3,4},{4,5},{5,6},{6,7},{8,9},{9,10},{10,11},{11... | collective-permute-start | bytes 3848 | tf_op jit(solution)/shard_map/ppermute | solution.py:17
  183.5 9.3 %collective-permute-start.21 = (bf16[64,10,1]{2,1,0:T(8,128)(2,1)S(1)}, bf16[64,10,1]{2,1,0:T(8,128)(2,1)S(1)}, u32[]{:S(2)}, u32[]{:S(2)}) collective-permute-start(bf16[64,10,1]{2,1,0:T(8,128)(2,1)S(1)} %get-tuple-element.167), channel_id=1, source_target_pairs={{1,0},{2,1},{3,2},{4,3},{5,4},{6,5},{7,6},{9,8},{10,9},{11,10},{12... | collective-permute-start | bytes 3848 | tf_op jit(solution)/shard_map/ppermute | solution.py:19
  194.1 4.4 collective-permute-start.22
  196.6 5.2 collective-permute-start.23
  202.2 8.3 %collective-permute-start.24 = (bf16[64,10,1]{2,1,0:T(8,128)(2,1)S(1)}, bf16[64,10,1]{2,1,0:T(8,128)(2,1)S(1)}, u32[]{:S(2)}, u32[]{:S(2)}) collective-permute-start(bf16[64,10,1]{2,1,0:T(8,128)(2,1)S(1)} %get-tuple-element.166), channel_id=1, source_target_pairs={{0,1},{1,2},{2,3},{3,4},{4,5},{5,6},{6,7},{8,9},{9,10},{10,11},{11... | collective-permute-start | bytes 3848 | tf_op jit(solution)/shard_map/ppermute | solution.py:17
  206.1 9.6 %collective-permute-start.25 = (bf16[64,10,1]{2,1,0:T(8,128)(2,1)S(1)}, bf16[64,10,1]{2,1,0:T(8,128)(2,1)S(1)}, u32[]{:S(2)}, u32[]{:S(2)}) collective-permute-start(bf16[64,10,1]{2,1,0:T(8,128)(2,1)S(1)} %get-tuple-element.165), channel_id=1, source_target_pairs={{1,0},{2,1},{3,2},{4,3},{5,4},{6,5},{7,6},{9,8},{10,9},{11,10},{12... | collective-permute-start | bytes 3848 | tf_op jit(solution)/shard_map/ppermute | solution.py:19
  217.8 6.1 %collective-permute-start.26 = (bf16[64,1,128]{2,1,0:T(2,128)(2,1)S(1)}, bf16[64,1,128]{2,1,0:T(2,128)(2,1)S(1)}, u32[]{:S(2)}, u32[]{:S(2)}) collective-permute-start(bf16[64,1,128]{2,1,0:T(2,128)(2,1)S(1)} %get-tuple-element.211), channel_id=1, source_target_pairs={{0,8},{8,16},{16,24},{24,32},{32,40},{40,48},{48,56},{1,9},{9,17},... | collective-permute-start | bytes 49160 | tf_op jit(solution)/shard_map/ppermute | solution.py:17
  221.9 5.2 collective-permute-start.27
  228.2 7.6 %collective-permute-start.28 = (bf16[64,10,1]{2,1,0:T(8,128)(2,1)}, bf16[64,10,1]{2,1,0:T(8,128)(2,1)}, u32[]{:S(2)}, u32[]{:S(2)}) collective-permute-start(bf16[64,10,1]{2,1,0:T(8,128)(2,1)} %get-tuple-element.164), channel_id=1, source_target_pairs={{0,1},{1,2},{2,3},{3,4},{4,5},{5,6},{6,7},{8,9},{9,10},{10,11},{11... | collective-permute-start | bytes 3848 | tf_op jit(solution)/shard_map/ppermute | solution.py:17
  231.7 8.7 %collective-permute-start.29 = (bf16[64,10,1]{2,1,0:T(8,128)(2,1)}, bf16[64,10,1]{2,1,0:T(8,128)(2,1)S(1)}, u32[]{:S(2)}, u32[]{:S(2)}) collective-permute-start(bf16[64,10,1]{2,1,0:T(8,128)(2,1)} %get-tuple-element.163), channel_id=1, source_target_pairs={{1,0},{2,1},{3,2},{4,3},{5,4},{6,5},{7,6},{9,8},{10,9},{11,10},{12... | collective-permute-start | bytes 3848 | tf_op jit(solution)/shard_map/ppermute | solution.py:19
  242.6 4.5 collective-permute-start.30
  245.0 5.2 collective-permute-start.31
  251.3 7.7 %collective-permute-start.32 = (bf16[64,10,1]{2,1,0:T(8,128)(2,1)}, bf16[64,10,1]{2,1,0:T(8,128)(2,1)}, u32[]{:S(2)}, u32[]{:S(2)}) collective-permute-start(bf16[64,10,1]{2,1,0:T(8,128)(2,1)} %get-tuple-element.162), channel_id=1, source_target_pairs={{0,1},{1,2},{2,3},{3,4},{4,5},{5,6},{6,7},{8,9},{9,10},{10,11},{11... | collective-permute-start | bytes 3848 | tf_op jit(solution)/shard_map/ppermute | solution.py:17
  255.7 8.7 %collective-permute-start.33 = (bf16[64,10,1]{2,1,0:T(8,128)(2,1)}, bf16[64,10,1]{2,1,0:T(8,128)(2,1)S(1)}, u32[]{:S(2)}, u32[]{:S(2)}) collective-permute-start(bf16[64,10,1]{2,1,0:T(8,128)(2,1)} %get-tuple-element.161), channel_id=1, source_target_pairs={{1,0},{2,1},{3,2},{4,3},{5,4},{6,5},{7,6},{9,8},{10,9},{11,10},{12... | collective-permute-start | bytes 3848 | tf_op jit(solution)/shard_map/ppermute | solution.py:19
  267.7 28.3 %copy-start.12 = (bf16[64,1024]{1,0:T(8,128)(2,1)}, bf16[64,1024]{1,0:T(8,128)(2,1)S(1)}, u32[]{:S(2)}) copy-start(bf16[64,1024]{1,0:T(8,128)(2,1)S(1)} %fusion.22) | copy-start | bytes 393220
  268.5 6.0 %collective-permute-start.34 = (bf16[64,1,128]{2,1,0:T(2,128)(2,1)}, bf16[64,1,128]{2,1,0:T(2,128)(2,1)S(1)}, u32[]{:S(2)}, u32[]{:S(2)}) collective-permute-start(bf16[64,1,128]{2,1,0:T(2,128)(2,1)} %get-tuple-element.207), channel_id=1, source_target_pairs={{0,8},{8,16},{16,24},{24,32},{32,40},{40,48},{48,56},{1,9},{9,17},... | collective-permute-start | bytes 49160 | tf_op jit(solution)/shard_map/ppermute | solution.py:17
  270.4 5.6 collective-permute-start.35
  277.7 8.7 %collective-permute-start.36 = (bf16[64,10,1]{2,1,0:T(8,128)(2,1)}, bf16[64,10,1]{2,1,0:T(8,128)(2,1)}, u32[]{:S(2)}, u32[]{:S(2)}) collective-permute-start(bf16[64,10,1]{2,1,0:T(8,128)(2,1)} %get-tuple-element.160), channel_id=1, source_target_pairs={{0,1},{1,2},{2,3},{3,4},{4,5},{5,6},{6,7},{8,9},{9,10},{10,11},{11... | collective-permute-start | bytes 3848 | tf_op jit(solution)/shard_map/ppermute | solution.py:17
  285.2 9.3 %collective-permute-start.37 = (bf16[64,10,1]{2,1,0:T(8,128)(2,1)}, bf16[64,10,1]{2,1,0:T(8,128)(2,1)S(1)}, u32[]{:S(2)}, u32[]{:S(2)}) collective-permute-start(bf16[64,10,1]{2,1,0:T(8,128)(2,1)} %get-tuple-element.159), channel_id=1, source_target_pairs={{1,0},{2,1},{3,2},{4,3},{5,4},{6,5},{7,6},{9,8},{10,9},{11,10},{12... | collective-permute-start | bytes 3848 | tf_op jit(solution)/shard_map/ppermute | solution.py:19
  298.8 9.9 %collective-permute-start.38 = (bf16[64,1,128]{2,1,0:T(2,128)(2,1)}, bf16[64,1,128]{2,1,0:T(2,128)(2,1)S(1)}, u32[]{:S(2)}, u32[]{:S(2)}) collective-permute-start(bf16[64,1,128]{2,1,0:T(2,128)(2,1)} %get-tuple-element.205), channel_id=1, source_target_pairs={{0,8},{8,16},{16,24},{24,32},{32,40},{40,48},{48,56},{1,9},{9,17},... | collective-permute-start | bytes 49160 | tf_op jit(solution)/shard_map/ppermute | solution.py:17
  300.7 8.0 %collective-permute-start.39 = (bf16[64,1,128]{2,1,0:T(2,128)(2,1)}, bf16[64,1,128]{2,1,0:T(2,128)(2,1)S(1)}, u32[]{:S(2)}, u32[]{:S(2)}) collective-permute-start(bf16[64,1,128]{2,1,0:T(2,128)(2,1)} %get-tuple-element.206), channel_id=1, source_target_pairs={{8,0},{16,8},{24,16},{32,24},{40,32},{48,40},{56,48},{9,1},{17,9},... | collective-permute-start | bytes 49160 | tf_op jit(solution)/shard_map/ppermute | solution.py:19
  309.0 8.4 %collective-permute-start.40 = (bf16[64,10,1]{2,1,0:T(8,128)(2,1)S(1)}, bf16[64,10,1]{2,1,0:T(8,128)(2,1)S(1)}, u32[]{:S(2)}, u32[]{:S(2)}) collective-permute-start(bf16[64,10,1]{2,1,0:T(8,128)(2,1)S(1)} %get-tuple-element.158), channel_id=1, source_target_pairs={{0,1},{1,2},{2,3},{3,4},{4,5},{5,6},{6,7},{8,9},{9,10},{10,11},{11... | collective-permute-start | bytes 3848 | tf_op jit(solution)/shard_map/ppermute | solution.py:17
  312.0 10.1 %collective-permute-start.41 = (bf16[64,10,1]{2,1,0:T(8,128)(2,1)S(1)}, bf16[64,10,1]{2,1,0:T(8,128)(2,1)S(1)}, u32[]{:S(2)}, u32[]{:S(2)}) collective-permute-start(bf16[64,10,1]{2,1,0:T(8,128)(2,1)S(1)} %get-tuple-element.157), channel_id=1, source_target_pairs={{1,0},{2,1},{3,2},{4,3},{5,4},{6,5},{7,6},{9,8},{10,9},{11,10},{12... | collective-permute-start | bytes 3848 | tf_op jit(solution)/shard_map/ppermute | solution.py:19
  324.3 4.8 collective-permute-start.42
  326.3 5.2 collective-permute-start.43
  331.8 8.0 %collective-permute-start.44 = (bf16[64,10,1]{2,1,0:T(8,128)(2,1)S(1)}, bf16[64,10,1]{2,1,0:T(8,128)(2,1)S(1)}, u32[]{:S(2)}, u32[]{:S(2)}) collective-permute-start(bf16[64,10,1]{2,1,0:T(8,128)(2,1)S(1)} %get-tuple-element.156), channel_id=1, source_target_pairs={{0,1},{1,2},{2,3},{3,4},{4,5},{5,6},{6,7},{8,9},{9,10},{10,11},{11... | collective-permute-start | bytes 3848 | tf_op jit(solution)/shard_map/ppermute | solution.py:17
  335.4 9.0 %collective-permute-start.45 = (bf16[64,10,1]{2,1,0:T(8,128)(2,1)S(1)}, bf16[64,10,1]{2,1,0:T(8,128)(2,1)S(1)}, u32[]{:S(2)}, u32[]{:S(2)}) collective-permute-start(bf16[64,10,1]{2,1,0:T(8,128)(2,1)S(1)} %get-tuple-element.155), channel_id=1, source_target_pairs={{1,0},{2,1},{3,2},{4,3},{5,4},{6,5},{7,6},{9,8},{10,9},{11,10},{12... | collective-permute-start | bytes 3848 | tf_op jit(solution)/shard_map/ppermute | solution.py:19
  346.6 4.8 collective-permute-start.46
  348.5 5.2 collective-permute-start.47
  354.0 7.8 %collective-permute-start.48 = (bf16[64,10,1]{2,1,0:T(8,128)(2,1)S(1)}, bf16[64,10,1]{2,1,0:T(8,128)(2,1)S(1)}, u32[]{:S(2)}, u32[]{:S(2)}) collective-permute-start(bf16[64,10,1]{2,1,0:T(8,128)(2,1)S(1)} %get-tuple-element.154), channel_id=1, source_target_pairs={{0,1},{1,2},{2,3},{3,4},{4,5},{5,6},{6,7},{8,9},{9,10},{10,11},{11... | collective-permute-start | bytes 3848 | tf_op jit(solution)/shard_map/ppermute | solution.py:17
  357.8 9.0 %collective-permute-start.49 = (bf16[64,10,1]{2,1,0:T(8,128)(2,1)S(1)}, bf16[64,10,1]{2,1,0:T(8,128)(2,1)S(1)}, u32[]{:S(2)}, u32[]{:S(2)}) collective-permute-start(bf16[64,10,1]{2,1,0:T(8,128)(2,1)S(1)} %get-tuple-element.153), channel_id=1, source_target_pairs={{1,0},{2,1},{3,2},{4,3},{5,4},{6,5},{7,6},{9,8},{10,9},{11,10},{12... | collective-permute-start | bytes 3848 | tf_op jit(solution)/shard_map/ppermute | solution.py:19
  369.6 11.9 %collective-permute-start.1 = (f32[64,1024]{1,0:T(8,128)S(1)}, f32[64,1024]{1,0:T(8,128)S(1)}, u32[]{:S(2)}, u32[]{:S(2)}) collective-permute-start(f32[64,1024]{1,0:T(8,128)S(1)} %convolution_add_fusion.5), channel_id=1, source_target_pairs={{64,0},{128,64},{192,128},{256,192},{320,256},{384,320},{448,384},... | collective-permute-start | bytes 786440 | tf_op jit(solution)/shard_map/while/body/eval_jaxpr/ppermute | solution.py:29
  381.9 12.0 %collective-permute-start.1 = (f32[64,1024]{1,0:T(8,128)S(1)}, f32[64,1024]{1,0:T(8,128)S(1)}, u32[]{:S(2)}, u32[]{:S(2)}) collective-permute-start(f32[64,1024]{1,0:T(8,128)S(1)} %convolution_add_fusion.5), channel_id=1, source_target_pairs={{64,0},{128,64},{192,128},{256,192},{320,256},{384,320},{448,384},... | collective-permute-start | bytes 786440 | tf_op jit(solution)/shard_map/while/body/eval_jaxpr/ppermute | solution.py:29
  394.3 11.4 %collective-permute-start.1 = (f32[64,1024]{1,0:T(8,128)S(1)}, f32[64,1024]{1,0:T(8,128)S(1)}, u32[]{:S(2)}, u32[]{:S(2)}) collective-permute-start(f32[64,1024]{1,0:T(8,128)S(1)} %convolution_add_fusion.5), channel_id=1, source_target_pairs={{64,0},{128,64},{192,128},{256,192},{320,256},{384,320},{448,384},... | collective-permute-start | bytes 786440 | tf_op jit(solution)/shard_map/while/body/eval_jaxpr/ppermute | solution.py:29
  406.0 10.3 %collective-permute-start.1 = (f32[64,1024]{1,0:T(8,128)S(1)}, f32[64,1024]{1,0:T(8,128)S(1)}, u32[]{:S(2)}, u32[]{:S(2)}) collective-permute-start(f32[64,1024]{1,0:T(8,128)S(1)} %convolution_add_fusion.5), channel_id=1, source_target_pairs={{64,0},{128,64},{192,128},{256,192},{320,256},{384,320},{448,384},... | collective-permute-start | bytes 786440 | tf_op jit(solution)/shard_map/while/body/eval_jaxpr/ppermute | solution.py:29
  416.7 7.7 %collective-permute-start.1 = (f32[64,1024]{1,0:T(8,128)S(1)}, f32[64,1024]{1,0:T(8,128)S(1)}, u32[]{:S(2)}, u32[]{:S(2)}) collective-permute-start(f32[64,1024]{1,0:T(8,128)S(1)} %convolution_add_fusion.5), channel_id=1, source_target_pairs={{64,0},{128,64},{192,128},{256,192},{320,256},{384,320},{448,384},... | collective-permute-start | bytes 786440 | tf_op jit(solution)/shard_map/while/body/eval_jaxpr/ppermute | solution.py:29
  424.8 7.1 %collective-permute-start.1 = (f32[64,1024]{1,0:T(8,128)S(1)}, f32[64,1024]{1,0:T(8,128)S(1)}, u32[]{:S(2)}, u32[]{:S(2)}) collective-permute-start(f32[64,1024]{1,0:T(8,128)S(1)} %convolution_add_fusion.5), channel_id=1, source_target_pairs={{64,0},{128,64},{192,128},{256,192},{320,256},{384,320},{448,384},... | collective-permute-start | bytes 786440 | tf_op jit(solution)/shard_map/while/body/eval_jaxpr/ppermute | solution.py:29
  432.2 8.1 %collective-permute-start.1 = (f32[64,1024]{1,0:T(8,128)S(1)}, f32[64,1024]{1,0:T(8,128)S(1)}, u32[]{:S(2)}, u32[]{:S(2)}) collective-permute-start(f32[64,1024]{1,0:T(8,128)S(1)} %convolution_add_fusion.5), channel_id=1, source_target_pairs={{64,0},{128,64},{192,128},{256,192},{320,256},{384,320},{448,384},... | collective-permute-start | bytes 786440 | tf_op jit(solution)/shard_map/while/body/eval_jaxpr/ppermute | solution.py:29
  (26 other events, 132.9 us)
Sparse Core Ops, SparseCore 0:
  357.9 193.3 all-reduce.1
where the time goes:
time: 563 us; the launch traced here: 560 us
  waiting for transfers between devices  312 us (55%)
  starting transfers between devices  164 us (29%)
  local copies, waits for them, and re-layouts  28.5 us (5%)
  other arithmetic  24.9 us (4%)
  between operations  16.1 us (3%)
  matrix products  13.7 us (2%)
    psum x1, waiting for transfers between devices, local(): weight_grads = lax.psum(jnp.stack(grad_list, 0), ('row', 'col'))  110 us
    ppermute x14, waiting for transfers between devices, from_behind(): return lax.ppermute(array, axis, pairs)  88.8 us
    ppermute x24, waiting for transfers between devices, with_halo(): lax.ppermute(head, axis, [((i + 1) % count, i) for i in range(ends)])  78.5 us
    ppermute x24, starting transfers between devices, with_halo(): lax.ppermute(tail, axis, [(i, (i + 1) % count) for i in range(ends)])  77.9 us
    ppermute x24, starting transfers between devices, with_halo(): lax.ppermute(head, axis, [((i + 1) % count, i) for i in range(ends)])  45.4 us
    ppermute x14, starting transfers between devices, from_behind(): return lax.ppermute(array, axis, pairs)  41.1 us
    ppermute x24, waiting for transfers between devices, with_halo(): lax.ppermute(tail, axis, [(i, (i + 1) % count) for i in range(ends)])  34.7 us
    concatenate x36, other arithmetic, with_halo(): jnp.concatenate([lax.ppermute(tail, axis, [(i, (i + 1) % count) for i in...  21.9 us
  transfers between devices with their start and end apart: 63, of which 49 were waited for; matrix products, arithmetic and copies ran while one was open for 5% of the time, Pallas kernels for 0%

commit v1 on v0

--- a/solution.py
+++ b/solution.py
@@ -1,9 +1,17 @@
+import functools
 import jax
 import jax.numpy as jnp
 from jax import lax
 from jax.sharding import PartitionSpec as P
 
 step_size = 0.2
+
+
+def note_the_routes_all(packet, which_axis, axis_id):
+    return jax.lax.psum(jax.lax.psum(packet, axis_name=which_axis), axis_id)
+
+
+levels_all_make = functools.partial(note_the_routes_all, which_axis="col", axis_id="row")
 
 
 def with_halo(cells, sides, width):
@@ -116,7 +124,7 @@
             preferred_element_type=jnp.float32,
         )
         adjoint = adjoint + back
-    weight_grads = lax.psum(jnp.stack(grad_list, 0), ("row", "col"))
+    weight_grads = levels_all_make(jnp.stack(grad_list, 0))
     transposed = coarse_map.T
     back_map = jnp.where(is_last, zero_map, transposed)
     back_offset = jnp.where(is_last, adjoint, adjoint - exact_dot(transposed, guess_flat))

time: 563 us -> 525 us (0.933)
  waiting for transfers between devices: 312 us -> 273 us
    psum x1 -> x2, waiting for transfers between devices: 110 us -> 73.7 us  [note_the_routes_all(): return jax.lax.psum(jax.lax.psum(packet, axis_name=which_axis), axis_id)]
  transfers between devices with their start and end apart: 63 -> 64, of which waited for: 49 -> 50; matrix products, arithmetic and copies ran while one was open for 5% -> 6% of each run, Pallas kernels for 0% -> 0%
where the time goes in v1:
time: 525 us; the launch traced here: 520 us
  waiting for transfers between devices  273 us (52%)
  starting transfers between devices  164 us (31%)
  local copies, waits for them, and re-layouts  28.5 us (5%)
  other arithmetic  23.8 us (5%)
  between operations  16.2 us (3%)
  matrix products  13.6 us (3%)
    ppermute x14, waiting for transfers between devices, from_behind(): return lax.ppermute(array, axis, pairs)  85.1 us
    ppermute x24, waiting for transfers between devices, with_halo(): lax.ppermute(head, axis, [((i + 1) % count, i) for i in range(ends)])  79.1 us
    ppermute x24, starting transfers between devices, with_halo(): lax.ppermute(tail, axis, [(i, (i + 1) % count) for i in range(ends)])  77.1 us
    psum x2, waiting for transfers between devices, note_the_routes_all(): return jax.lax.psum(jax.lax.psum(packet, axis_name=which_axis), axis_id)  73.7 us
    ppermute x24, starting transfers between devices, with_halo(): lax.ppermute(head, axis, [((i + 1) % count, i) for i in range(ends)])  45.3 us
    ppermute x14, starting transfers between devices, from_behind(): return lax.ppermute(array, axis, pairs)  41.3 us
    ppermute x24, waiting for transfers between devices, with_halo(): lax.ppermute(tail, axis, [(i, (i + 1) % count) for i in range(ends)])  35.5 us
    concatenate x36, other arithmetic, with_halo(): jnp.concatenate([lax.ppermute(tail, axis, [(i, (i + 1) % count) for i in...  20.8 us
  transfers between devices with their start and end apart: 64, of which 50 were waited for; matrix products, arithmetic and copies ran while one was open for 6% of the time, Pallas kernels for 0%

profile of v1, /device:TPU:1, one launch (start us, length us, event | category | flops | bytes accessed | tf_op | source)
XLA Modules:
  0.0 519.5 jit_solution(5315430859390355206)
XLA Ops:
  8.2 4.5 collective-permute-start.2
  12.8 5.6 %collective-permute-start.3 = (bf16[64,1,128]{2,1,0:T(2,128)(2,1)S(1)}, bf16[64,1,128]{2,1,0:T(2,128)(2,1)S(1)}, u32[]{:S(2)}, u32[]{:S(2)}) collective-permute-start(bf16[64,1,128]{2,1,0:T(2,128)(2,1)S(1)} %get-tuple-element.224), channel_id=1, source_target_pairs={{8,0},{16,8},{24,16},{32,24},{40,32},{48,40},{56,48},{9,1},{17,9},... | collective-permute-start | bytes 49160 | tf_op jit(solution)/shard_map/ppermute | solution.py:27
  22.8 4.6 collective-permute-done.4
  27.9 3.7 collective-permute-done.5
  38.6 3.3 collective-permute-done.7
  42.2 3.2 collective-permute-start.8
  46.7 3.1 collective-permute-done.8
  50.3 3.6 collective-permute-done.9
  55.3 3.9 collective-permute-start.10
  61.1 3.3 collective-permute-done.11
  64.7 5.2 %collective-permute-start.12 = (bf16[64,10,1]{2,1,0:T(8,128)(2,1)S(1)}, bf16[64,10,1]{2,1,0:T(8,128)(2,1)S(1)}, u32[]{:S(2)}, u32[]{:S(2)}) collective-permute-start(bf16[64,10,1]{2,1,0:T(8,128)(2,1)S(1)} %get-tuple-element.172), channel_id=1, source_target_pairs={{0,1},{1,2},{2,3},{3,4},{4,5},{5,6},{6,7},{8,9},{9,10},{10,11},{11... | collective-permute-start | bytes 3848 | tf_op jit(solution)/shard_map/ppermute | solution.py:25
  74.9 4.8 collective-permute-done.13
  81.0 4.5 collective-permute-start.14
  87.6 3.2 collective-permute-done.15
  91.1 3.8 collective-permute-start.16
  96.3 3.0 collective-permute-done.16
  99.8 3.7 collective-permute-done.17
  105.2 64.1 %while.20 = (s32[]{:T(128)}, f32[64,1024]{1,0:T(8,128)S(1)}, f32[64,64]{1,0:T(8,128)S(1)}, f32[64,1024]{1,0:T(8,128)S(1)}, s32[]{:T(128)}) while((s32[]{:T(128)}, f32[64,1024]{1,0:T(8,128)S(1)}, f32[64,64]{1,0:T(8,128)S(1)}, f32[64,1024]{1,0:T(8,128)S(1)}, s32[]{:T(128)}) %tuple.143), condition=%wide.region_2.3_spmd, body=%wide.region_1.2_spmd.sunk | while | flops 50397184 | bytes 1851493 | solution.py:99
  105.6 4.0 collective-permute-start
  109.6 5.8 %collective-permute-done = f32[64,1024]{1,0:T(8,128)S(1)} collective-permute-done((f32[64,1024]{1,0:T(8,128)S(1)}, f32[64,1024]{1,0:T(8,128)S(1)}, u32[]{:S(2)}, u32[]{:S(2)}) %collective-permute-start) | collective-permute-done | bytes 262176 | tf_op jit(solution)/shard_map/while/body/eval_jaxpr/ppermute | solution.py:37
  115.8 4.0 collective-permute-start
  119.8 5.4 %collective-permute-done = f32[64,1024]{1,0:T(8,128)S(1)} collective-permute-done((f32[64,1024]{1,0:T(8,128)S(1)}, f32[64,1024]{1,0:T(8,128)S(1)}, u32[]{:S(2)}, u32[]{:S(2)}) %collective-permute-start) | collective-permute-done | bytes 262176 | tf_op jit(solution)/shard_map/while/body/eval_jaxpr/ppermute | solution.py:37
  125.6 4.1 collective-permute-start
  129.7 4.5 collective-permute-done
  134.6 5.4 %collective-permute-start = (f32[64,1024]{1,0:T(8,128)S(1)}, f32[64,1024]{1,0:T(8,128)S(1)}, u32[]{:S(2)}, u32[]{:S(2)}) collective-permute-start(f32[64,1024]{1,0:T(8,128)S(1)} %convolution_add_fusion.4), channel_id=1, source_target_pairs={{0,64},{64,128},{128,192},{192,256},{256,320},{320,384},{384,448},... | collective-permute-start | bytes 786440 | tf_op jit(solution)/shard_map/while/body/eval_jaxpr/ppermute | solution.py:37
  140.0 3.7 collective-permute-done
  144.1 4.1 collective-permute-start
  148.2 3.3 collective-permute-done
  151.8 5.3 %collective-permute-start = (f32[64,1024]{1,0:T(8,128)S(1)}, f32[64,1024]{1,0:T(8,128)S(1)}, u32[]{:S(2)}, u32[]{:S(2)}) collective-permute-start(f32[64,1024]{1,0:T(8,128)S(1)} %convolution_add_fusion.4), channel_id=1, source_target_pairs={{0,64},{64,128},{128,192},{192,256},{256,320},{320,384},{384,448},... | collective-permute-start | bytes 786440 | tf_op jit(solution)/shard_map/while/body/eval_jaxpr/ppermute | solution.py:37
  157.1 3.3 collective-permute-done
  160.8 5.3 %collective-permute-start = (f32[64,1024]{1,0:T(8,128)S(1)}, f32[64,1024]{1,0:T(8,128)S(1)}, u32[]{:S(2)}, u32[]{:S(2)}) collective-permute-start(f32[64,1024]{1,0:T(8,128)S(1)} %convolution_add_fusion.4), channel_id=1, source_target_pairs={{0,64},{64,128},{128,192},{192,256},{256,320},{320,384},{384,448},... | collective-permute-start | bytes 786440 | tf_op jit(solution)/shard_map/while/body/eval_jaxpr/ppermute | solution.py:37
  166.1 3.3 collective-permute-done
  169.5 6.1 %collective-permute-start.18 = (bf16[64,1,128]{2,1,0:T(2,128)(2,1)S(1)}, bf16[64,1,128]{2,1,0:T(2,128)(2,1)S(1)}, u32[]{:S(2)}, u32[]{:S(2)}) collective-permute-start(bf16[64,1,128]{2,1,0:T(2,128)(2,1)S(1)} %get-tuple-element.215), channel_id=1, source_target_pairs={{0,8},{8,16},{16,24},{24,32},{32,40},{40,48},{48,56},{1,9},{9,17},... | collective-permute-start | bytes 49160 | tf_op jit(solution)/shard_map/ppermute | solution.py:25
  184.8 3.9 collective-permute-done.20
  189.2 3.6 collective-permute-done.21
  198.6 3.3 collective-permute-done.23
  202.2 3.8 collective-permute-start.24
  207.3 3.1 collective-permute-done.24
  210.9 4.8 collective-permute-done.25
  217.9 4.0 collective-permute-start.26
  223.8 3.3 collective-permute-done.27
  228.1 3.1 collective-permute-start.28
  232.6 3.4 collective-permute-done.28
  236.5 3.5 collective-permute-done.29
  246.6 3.1 collective-permute-done.31
  250.8 3.9 collective-permute-start.32
  260.5 3.8 collective-permute-done.33
  277.5 3.4 collective-permute-start.36
  288.0 6.2 %collective-permute-done.37 = bf16[64,10,1]{2,1,0:T(8,128)(2,1)S(1)} collective-permute-done((bf16[64,10,1]{2,1,0:T(8,128)(2,1)}, bf16[64,10,1]{2,1,0:T(8,128)(2,1)S(1)}, u32[]{:S(2)}, u32[]{:S(2)}) %collective-permute-start.37) | collective-permute-done | bytes 1312 | tf_op jit(solution)/shard_map/ppermute | solution.py:27
  313.1 4.2 collective-permute-done.40
  317.8 3.9 collective-permute-done.41
  336.1 3.1 collective-permute-done.44
  339.7 4.1 collective-permute-done.45
  361.7 4.6 collective-permute-done.49
  368.6 65.9 %all-reduce.3.cloned.1.call-done = f32[4,64,576]{2,1,0:T(8,128)} async-done(((f32[4,64,576]{2,1,0:T(8,128)}), f32[4,64,576]{2,1,0:T(8,128)}) %all-reduce.3.cloned.1.call-update) | async-done | bytes 589840 | tf_op jit(solution)/shard_map/psum | solution.py:11
  434.6 67.5 %while.21 = (s32[]{:T(128)}, f32[64,1024]{1,0:T(8,128)S(1)}, f32[64,64]{1,0:T(8,128)S(1)}, f32[64,1024]{1,0:T(8,128)S(1)}, s32[]{:T(128)}) while((s32[]{:T(128)}, f32[64,1024]{1,0:T(8,128)S(1)}, f32[64,64]{1,0:T(8,128)S(1)}, f32[64,1024]{1,0:T(8,128)S(1)}, s32[]{:T(128)}) %tuple.146), condition=%wide.region_4.5_spmd, body=%wide.region_3.4_spmd.sunk | while | flops 50397184 | bytes 1851493 | solution.py:135
  436.3 5.8 %collective-permute-done.1 = f32[64,1024]{1,0:T(8,128)S(1)} collective-permute-done((f32[64,1024]{1,0:T(8,128)S(1)}, f32[64,1024]{1,0:T(8,128)S(1)}, u32[]{:S(2)}, u32[]{:S(2)}) %collective-permute-start.1) | collective-permute-done | bytes 262176 | tf_op jit(solution)/shard_map/while/body/eval_jaxpr/ppermute | solution.py:37
  443.8 6.8 %collective-permute-done.1 = f32[64,1024]{1,0:T(8,128)S(1)} collective-permute-done((f32[64,1024]{1,0:T(8,128)S(1)}, f32[64,1024]{1,0:T(8,128)S(1)}, u32[]{:S(2)}, u32[]{:S(2)}) %collective-permute-start.1) | collective-permute-done | bytes 262176 | tf_op jit(solution)/shard_map/while/body/eval_jaxpr/ppermute | solution.py:37
  452.2 8.3 %collective-permute-done.1 = f32[64,1024]{1,0:T(8,128)S(1)} collective-permute-done((f32[64,1024]{1,0:T(8,128)S(1)}, f32[64,1024]{1,0:T(8,128)S(1)}, u32[]{:S(2)}, u32[]{:S(2)}) %collective-permute-start.1) | collective-permute-done | bytes 262176 | tf_op jit(solution)/shard_map/while/body/eval_jaxpr/ppermute | solution.py:37
  462.2 8.9 %collective-permute-done.1 = f32[64,1024]{1,0:T(8,128)S(1)} collective-permute-done((f32[64,1024]{1,0:T(8,128)S(1)}, f32[64,1024]{1,0:T(8,128)S(1)}, u32[]{:S(2)}, u32[]{:S(2)}) %collective-permute-start.1) | collective-permute-done | bytes 262176 | tf_op jit(solution)/shard_map/while/body/eval_jaxpr/ppermute | solution.py:37
  472.7 8.0 %collective-permute-done.1 = f32[64,1024]{1,0:T(8,128)S(1)} collective-permute-done((f32[64,1024]{1,0:T(8,128)S(1)}, f32[64,1024]{1,0:T(8,128)S(1)}, u32[]{:S(2)}, u32[]{:S(2)}) %collective-permute-start.1) | collective-permute-done | bytes 262176 | tf_op jit(solution)/shard_map/while/body/eval_jaxpr/ppermute | solution.py:37
  482.4 8.0 %collective-permute-done.1 = f32[64,1024]{1,0:T(8,128)S(1)} collective-permute-done((f32[64,1024]{1,0:T(8,128)S(1)}, f32[64,1024]{1,0:T(8,128)S(1)}, u32[]{:S(2)}, u32[]{:S(2)}) %collective-permute-start.1) | collective-permute-done | bytes 262176 | tf_op jit(solution)/shard_map/while/body/eval_jaxpr/ppermute | solution.py:37
  492.1 10.1 %collective-permute-done.1 = f32[64,1024]{1,0:T(8,128)S(1)} collective-permute-done((f32[64,1024]{1,0:T(8,128)S(1)}, f32[64,1024]{1,0:T(8,128)S(1)}, u32[]{:S(2)}, u32[]{:S(2)}) %collective-permute-start.1) | collective-permute-done | bytes 262176 | tf_op jit(solution)/shard_map/while/body/eval_jaxpr/ppermute | solution.py:37
  503.0 7.7 %all-reduce.5.cloned.1.call-done = f32[4,64,576]{2,1,0:T(8,128)} async-done(((f32[4,64,576]{2,1,0:T(8,128)}), f32[4,64,576]{2,1,0:T(8,128)}) %all-reduce.5.cloned.1.call-update) | async-done | bytes 589840 | tf_op jit(solution)/shard_map/psum | solution.py:11
  (363 shorter events, 158.7 us)
Async XLA Ops:
  7.2 427.4 %all-reduce.3.cloned.1.call-start = ((), (), s32[]{:S(2)}) async-start(), calls=%async_computation | async-start | bytes 1310720 | tf_op jit(solution)/shard_map/psum | solution.py:11
  8.2 10.1 %collective-permute-start.2 = (bf16[64,1,128]{2,1,0:T(2,128)(2,1)S(1)}, bf16[64,1,128]{2,1,0:T(2,128)(2,1)S(1)}, u32[]{:S(2)}, u32[]{:S(2)}) collective-permute-start(bf16[64,1,128]{2,1,0:T(2,128)(2,1)S(1)} %get-tuple-element.223), channel_id=1, source_target_pairs={{0,8},{8,16},{16,24},{24,32},{32,40},{40,48},{48,56},{1,9},{9,17},... | collective-permute-start | bytes 49160 | tf_op jit(solution)/shard_map/ppermute | solution.py:25
  12.8 6.4 %collective-permute-start.3 = (bf16[64,1,128]{2,1,0:T(2,128)(2,1)S(1)}, bf16[64,1,128]{2,1,0:T(2,128)(2,1)S(1)}, u32[]{:S(2)}, u32[]{:S(2)}) collective-permute-start(bf16[64,1,128]{2,1,0:T(2,128)(2,1)S(1)} %get-tuple-element.224), channel_id=1, source_target_pairs={{8,0},{16,8},{24,16},{32,24},{40,32},{48,40},{56,48},{9,1},{17,9},... | collective-permute-start | bytes 49160 | tf_op jit(solution)/shard_map/ppermute | solution.py:27
  19.5 7.9 %collective-permute-start.4 = (bf16[64,10,1]{2,1,0:T(8,128)(2,1)S(1)}, bf16[64,10,1]{2,1,0:T(8,128)(2,1)S(1)}, u32[]{:S(2)}, u32[]{:S(2)}) collective-permute-start(bf16[64,10,1]{2,1,0:T(8,128)(2,1)S(1)} %get-tuple-element.176), channel_id=1, source_target_pairs={{0,1},{1,2},{2,3},{3,4},{4,5},{5,6},{6,7},{8,9},{9,10},{10,11},{11... | collective-permute-start | bytes 3848 | tf_op jit(solution)/shard_map/ppermute | solution.py:25
  21.5 10.1 %collective-permute-start.5 = (bf16[64,10,1]{2,1,0:T(8,128)(2,1)S(1)}, bf16[64,10,1]{2,1,0:T(8,128)(2,1)S(1)}, u32[]{:S(2)}, u32[]{:S(2)}) collective-permute-start(bf16[64,10,1]{2,1,0:T(8,128)(2,1)S(1)} %get-tuple-element.175), channel_id=1, source_target_pairs={{1,0},{2,1},{3,2},{4,3},{5,4},{6,5},{7,6},{9,8},{10,9},{11,10},{12... | collective-permute-start | bytes 3848 | tf_op jit(solution)/shard_map/ppermute | solution.py:27
  33.8 4.8 collective-permute-start.6
  36.7 5.2 %collective-permute-start.7 = (bf16[64,1,128]{2,1,0:T(2,128)(2,1)S(1)}, bf16[64,1,128]{2,1,0:T(2,128)(2,1)S(1)}, u32[]{:S(2)}, u32[]{:S(2)}) collective-permute-start(bf16[64,1,128]{2,1,0:T(2,128)(2,1)S(1)} %get-tuple-element.222), channel_id=1, source_target_pairs={{8,0},{16,8},{24,16},{32,24},{40,32},{48,40},{56,48},{9,1},{17,9},... | collective-permute-start | bytes 49160 | tf_op jit(solution)/shard_map/ppermute | solution.py:27
  42.2 7.6 %collective-permute-start.8 = (bf16[64,10,1]{2,1,0:T(8,128)(2,1)S(1)}, bf16[64,10,1]{2,1,0:T(8,128)(2,1)S(1)}, u32[]{:S(2)}, u32[]{:S(2)}) collective-permute-start(bf16[64,10,1]{2,1,0:T(8,128)(2,1)S(1)} %get-tuple-element.174), channel_id=1, source_target_pairs={{0,1},{1,2},{2,3},{3,4},{4,5},{5,6},{6,7},{8,9},{9,10},{10,11},{11... | collective-permute-start | bytes 3848 | tf_op jit(solution)/shard_map/ppermute | solution.py:25
  45.4 8.6 %collective-permute-start.9 = (bf16[64,10,1]{2,1,0:T(8,128)(2,1)S(1)}, bf16[64,10,1]{2,1,0:T(8,128)(2,1)S(1)}, u32[]{:S(2)}, u32[]{:S(2)}) collective-permute-start(bf16[64,10,1]{2,1,0:T(8,128)(2,1)S(1)} %get-tuple-element.173), channel_id=1, source_target_pairs={{1,0},{2,1},{3,2},{4,3},{5,4},{6,5},{7,6},{9,8},{10,9},{11,10},{12... | collective-permute-start | bytes 3848 | tf_op jit(solution)/shard_map/ppermute | solution.py:27
  55.3 5.8 %collective-permute-start.10 = (bf16[64,1,128]{2,1,0:T(2,128)(2,1)S(1)}, bf16[64,1,128]{2,1,0:T(2,128)(2,1)S(1)}, u32[]{:S(2)}, u32[]{:S(2)}) collective-permute-start(bf16[64,1,128]{2,1,0:T(2,128)(2,1)S(1)} %get-tuple-element.219), channel_id=1, source_target_pairs={{0,8},{8,16},{16,24},{24,32},{32,40},{40,48},{48,56},{1,9},{9,17},... | collective-permute-start | bytes 49160 | tf_op jit(solution)/shard_map/ppermute | solution.py:25
  59.2 5.2 %collective-permute-start.11 = (bf16[64,1,128]{2,1,0:T(2,128)(2,1)S(1)}, bf16[64,1,128]{2,1,0:T(2,128)(2,1)S(1)}, u32[]{:S(2)}, u32[]{:S(2)}) collective-permute-start(bf16[64,1,128]{2,1,0:T(2,128)(2,1)S(1)} %get-tuple-element.220), channel_id=1, source_target_pairs={{8,0},{16,8},{24,16},{32,24},{40,32},{48,40},{56,48},{9,1},{17,9},... | collective-permute-start | bytes 49160 | tf_op jit(solution)/shard_map/ppermute | solution.py:27
  64.7 9.7 %collective-permute-start.12 = (bf16[64,10,1]{2,1,0:T(8,128)(2,1)S(1)}, bf16[64,10,1]{2,1,0:T(8,128)(2,1)S(1)}, u32[]{:S(2)}, u32[]{:S(2)}) collective-permute-start(bf16[64,10,1]{2,1,0:T(8,128)(2,1)S(1)} %get-tuple-element.172), channel_id=1, source_target_pairs={{0,1},{1,2},{2,3},{3,4},{4,5},{5,6},{6,7},{8,9},{9,10},{10,11},{11... | collective-permute-start | bytes 3848 | tf_op jit(solution)/shard_map/ppermute | solution.py:25
  70.8 8.9 %collective-permute-start.13 = (bf16[64,10,1]{2,1,0:T(8,128)(2,1)S(1)}, bf16[64,10,1]{2,1,0:T(8,128)(2,1)S(1)}, u32[]{:S(2)}, u32[]{:S(2)}) collective-permute-start(bf16[64,10,1]{2,1,0:T(8,128)(2,1)S(1)} %get-tuple-element.171), channel_id=1, source_target_pairs={{1,0},{2,1},{3,2},{4,3},{5,4},{6,5},{7,6},{9,8},{10,9},{11,10},{12... | collective-permute-start | bytes 3848 | tf_op jit(solution)/shard_map/ppermute | solution.py:27
  81.0 6.5 %collective-permute-start.14 = (bf16[64,1,128]{2,1,0:T(2,128)(2,1)S(1)}, bf16[64,1,128]{2,1,0:T(2,128)(2,1)S(1)}, u32[]{:S(2)}, u32[]{:S(2)}) collective-permute-start(bf16[64,1,128]{2,1,0:T(2,128)(2,1)S(1)} %get-tuple-element.217), channel_id=1, source_target_pairs={{0,8},{8,16},{16,24},{24,32},{32,40},{40,48},{48,56},{1,9},{9,17},... | collective-permute-start | bytes 49160 | tf_op jit(solution)/shard_map/ppermute | solution.py:25
  85.6 5.2 %collective-permute-start.15 = (bf16[64,1,128]{2,1,0:T(2,128)(2,1)S(1)}, bf16[64,1,128]{2,1,0:T(2,128)(2,1)S(1)}, u32[]{:S(2)}, u32[]{:S(2)}) collective-permute-start(bf16[64,1,128]{2,1,0:T(2,128)(2,1)S(1)} %get-tuple-element.218), channel_id=1, source_target_pairs={{8,0},{16,8},{24,16},{32,24},{40,32},{48,40},{56,48},{9,1},{17,9},... | collective-permute-start | bytes 49160 | tf_op jit(solution)/shard_map/ppermute | solution.py:27
  91.1 8.2 %collective-permute-start.16 = (bf16[64,10,1]{2,1,0:T(8,128)(2,1)S(1)}, bf16[64,10,1]{2,1,0:T(8,128)(2,1)S(1)}, u32[]{:S(2)}, u32[]{:S(2)}) collective-permute-start(bf16[64,10,1]{2,1,0:T(8,128)(2,1)S(1)} %get-tuple-element.170), channel_id=1, source_target_pairs={{0,1},{1,2},{2,3},{3,4},{4,5},{5,6},{6,7},{8,9},{9,10},{10,11},{11... | collective-permute-start | bytes 3848 | tf_op jit(solution)/shard_map/ppermute | solution.py:25
  95.0 8.5 %collective-permute-start.17 = (bf16[64,10,1]{2,1,0:T(8,128)(2,1)S(1)}, bf16[64,10,1]{2,1,0:T(8,128)(2,1)S(1)}, u32[]{:S(2)}, u32[]{:S(2)}) collective-permute-start(bf16[64,10,1]{2,1,0:T(8,128)(2,1)S(1)} %get-tuple-element.169), channel_id=1, source_target_pairs={{1,0},{2,1},{3,2},{4,3},{5,4},{6,5},{7,6},{9,8},{10,9},{11,10},{12... | collective-permute-start | bytes 3848 | tf_op jit(solution)/shard_map/ppermute | solution.py:27
  105.6 9.8 %collective-permute-start = (f32[64,1024]{1,0:T(8,128)S(1)}, f32[64,1024]{1,0:T(8,128)S(1)}, u32[]{:S(2)}, u32[]{:S(2)}) collective-permute-start(f32[64,1024]{1,0:T(8,128)S(1)} %convolution_add_fusion.4), channel_id=1, source_target_pairs={{0,64},{64,128},{128,192},{192,256},{256,320},{320,384},{384,448},... | collective-permute-start | bytes 786440 | tf_op jit(solution)/shard_map/while/body/eval_jaxpr/ppermute | solution.py:37
  115.8 9.4 %collective-permute-start = (f32[64,1024]{1,0:T(8,128)S(1)}, f32[64,1024]{1,0:T(8,128)S(1)}, u32[]{:S(2)}, u32[]{:S(2)}) collective-permute-start(f32[64,1024]{1,0:T(8,128)S(1)} %convolution_add_fusion.4), channel_id=1, source_target_pairs={{0,64},{64,128},{128,192},{192,256},{256,320},{320,384},{384,448},... | collective-permute-start | bytes 786440 | tf_op jit(solution)/shard_map/while/body/eval_jaxpr/ppermute | solution.py:37
  125.6 8.6 %collective-permute-start = (f32[64,1024]{1,0:T(8,128)S(1)}, f32[64,1024]{1,0:T(8,128)S(1)}, u32[]{:S(2)}, u32[]{:S(2)}) collective-permute-start(f32[64,1024]{1,0:T(8,128)S(1)} %convolution_add_fusion.4), channel_id=1, source_target_pairs={{0,64},{64,128},{128,192},{192,256},{256,320},{320,384},{384,448},... | collective-permute-start | bytes 786440 | tf_op jit(solution)/shard_map/while/body/eval_jaxpr/ppermute | solution.py:37
  134.6 9.1 %collective-permute-start = (f32[64,1024]{1,0:T(8,128)S(1)}, f32[64,1024]{1,0:T(8,128)S(1)}, u32[]{:S(2)}, u32[]{:S(2)}) collective-permute-start(f32[64,1024]{1,0:T(8,128)S(1)} %convolution_add_fusion.4), channel_id=1, source_target_pairs={{0,64},{64,128},{128,192},{192,256},{256,320},{320,384},{384,448},... | collective-permute-start | bytes 786440 | tf_op jit(solution)/shard_map/while/body/eval_jaxpr/ppermute | solution.py:37
  144.1 7.4 %collective-permute-start = (f32[64,1024]{1,0:T(8,128)S(1)}, f32[64,1024]{1,0:T(8,128)S(1)}, u32[]{:S(2)}, u32[]{:S(2)}) collective-permute-start(f32[64,1024]{1,0:T(8,128)S(1)} %convolution_add_fusion.4), channel_id=1, source_target_pairs={{0,64},{64,128},{128,192},{192,256},{256,320},{320,384},{384,448},... | collective-permute-start | bytes 786440 | tf_op jit(solution)/shard_map/while/body/eval_jaxpr/ppermute | solution.py:37
  151.8 8.6 %collective-permute-start = (f32[64,1024]{1,0:T(8,128)S(1)}, f32[64,1024]{1,0:T(8,128)S(1)}, u32[]{:S(2)}, u32[]{:S(2)}) collective-permute-start(f32[64,1024]{1,0:T(8,128)S(1)} %convolution_add_fusion.4), channel_id=1, source_target_pairs={{0,64},{64,128},{128,192},{192,256},{256,320},{320,384},{384,448},... | collective-permute-start | bytes 786440 | tf_op jit(solution)/shard_map/while/body/eval_jaxpr/ppermute | solution.py:37
  160.8 8.6 %collective-permute-start = (f32[64,1024]{1,0:T(8,128)S(1)}, f32[64,1024]{1,0:T(8,128)S(1)}, u32[]{:S(2)}, u32[]{:S(2)}) collective-permute-start(f32[64,1024]{1,0:T(8,128)S(1)} %convolution_add_fusion.4), channel_id=1, source_target_pairs={{0,64},{64,128},{128,192},{192,256},{256,320},{320,384},{384,448},... | collective-permute-start | bytes 786440 | tf_op jit(solution)/shard_map/while/body/eval_jaxpr/ppermute | solution.py:37
  169.5 9.0 %collective-permute-start.18 = (bf16[64,1,128]{2,1,0:T(2,128)(2,1)S(1)}, bf16[64,1,128]{2,1,0:T(2,128)(2,1)S(1)}, u32[]{:S(2)}, u32[]{:S(2)}) collective-permute-start(bf16[64,1,128]{2,1,0:T(2,128)(2,1)S(1)} %get-tuple-element.215), channel_id=1, source_target_pairs={{0,8},{8,16},{16,24},{24,32},{32,40},{40,48},{48,56},{1,9},{9,17},... | collective-permute-start | bytes 49160 | tf_op jit(solution)/shard_map/ppermute | solution.py:25
  175.6 5.2 %collective-permute-start.19 = (bf16[64,1,128]{2,1,0:T(2,128)(2,1)S(1)}, bf16[64,1,128]{2,1,0:T(2,128)(2,1)S(1)}, u32[]{:S(2)}, u32[]{:S(2)}) collective-permute-start(bf16[64,1,128]{2,1,0:T(2,128)(2,1)S(1)} %get-tuple-element.216), channel_id=1, source_target_pairs={{8,0},{16,8},{24,16},{32,24},{40,32},{48,40},{56,48},{9,1},{17,9},... | collective-permute-start | bytes 49160 | tf_op jit(solution)/shard_map/ppermute | solution.py:27
  181.2 7.5 %collective-permute-start.20 = (bf16[64,10,1]{2,1,0:T(8,128)(2,1)S(1)}, bf16[64,10,1]{2,1,0:T(8,128)(2,1)S(1)}, u32[]{:S(2)}, u32[]{:S(2)}) collective-permute-start(bf16[64,10,1]{2,1,0:T(8,128)(2,1)S(1)} %get-tuple-element.168), channel_id=1, source_target_pairs={{0,1},{1,2},{2,3},{3,4},{4,5},{5,6},{6,7},{8,9},{9,10},{10,11},{11... | collective-permute-start | bytes 3848 | tf_op jit(solution)/shard_map/ppermute | solution.py:25
  183.3 9.5 %collective-permute-start.21 = (bf16[64,10,1]{2,1,0:T(8,128)(2,1)S(1)}, bf16[64,10,1]{2,1,0:T(8,128)(2,1)S(1)}, u32[]{:S(2)}, u32[]{:S(2)}) collective-permute-start(bf16[64,10,1]{2,1,0:T(8,128)(2,1)S(1)} %get-tuple-element.167), channel_id=1, source_target_pairs={{1,0},{2,1},{3,2},{4,3},{5,4},{6,5},{7,6},{9,8},{10,9},{11,10},{12... | collective-permute-start | bytes 3848 | tf_op jit(solution)/shard_map/ppermute | solution.py:27
  194.2 4.4 collective-permute-start.22
  196.6 5.2 %collective-permute-start.23 = (bf16[64,1,128]{2,1,0:T(2,128)(2,1)S(1)}, bf16[64,1,128]{2,1,0:T(2,128)(2,1)S(1)}, u32[]{:S(2)}, u32[]{:S(2)}) collective-permute-start(bf16[64,1,128]{2,1,0:T(2,128)(2,1)S(1)} %get-tuple-element.214), channel_id=1, source_target_pairs={{8,0},{16,8},{24,16},{32,24},{40,32},{48,40},{56,48},{9,1},{17,9},... | collective-permute-start | bytes 49160 | tf_op jit(solution)/shard_map/ppermute | solution.py:27
  202.2 8.2 %collective-permute-start.24 = (bf16[64,10,1]{2,1,0:T(8,128)(2,1)S(1)}, bf16[64,10,1]{2,1,0:T(8,128)(2,1)S(1)}, u32[]{:S(2)}, u32[]{:S(2)}) collective-permute-start(bf16[64,10,1]{2,1,0:T(8,128)(2,1)S(1)} %get-tuple-element.166), channel_id=1, source_target_pairs={{0,1},{1,2},{2,3},{3,4},{4,5},{5,6},{6,7},{8,9},{9,10},{10,11},{11... | collective-permute-start | bytes 3848 | tf_op jit(solution)/shard_map/ppermute | solution.py:25
  206.0 9.8 %collective-permute-start.25 = (bf16[64,10,1]{2,1,0:T(8,128)(2,1)S(1)}, bf16[64,10,1]{2,1,0:T(8,128)(2,1)S(1)}, u32[]{:S(2)}, u32[]{:S(2)}) collective-permute-start(bf16[64,10,1]{2,1,0:T(8,128)(2,1)S(1)} %get-tuple-element.165), channel_id=1, source_target_pairs={{1,0},{2,1},{3,2},{4,3},{5,4},{6,5},{7,6},{9,8},{10,9},{11,10},{12... | collective-permute-start | bytes 3848 | tf_op jit(solution)/shard_map/ppermute | solution.py:27
  217.9 5.9 %collective-permute-start.26 = (bf16[64,1,128]{2,1,0:T(2,128)(2,1)S(1)}, bf16[64,1,128]{2,1,0:T(2,128)(2,1)S(1)}, u32[]{:S(2)}, u32[]{:S(2)}) collective-permute-start(bf16[64,1,128]{2,1,0:T(2,128)(2,1)S(1)} %get-tuple-element.211), channel_id=1, source_target_pairs={{0,8},{8,16},{16,24},{24,32},{32,40},{40,48},{48,56},{1,9},{9,17},... | collective-permute-start | bytes 49160 | tf_op jit(solution)/shard_map/ppermute | solution.py:25
  221.8 5.2 %collective-permute-start.27 = (bf16[64,1,128]{2,1,0:T(2,128)(2,1)S(1)}, bf16[64,1,128]{2,1,0:T(2,128)(2,1)S(1)}, u32[]{:S(2)}, u32[]{:S(2)}) collective-permute-start(bf16[64,1,128]{2,1,0:T(2,128)(2,1)S(1)} %get-tuple-element.212), channel_id=1, source_target_pairs={{8,0},{16,8},{24,16},{32,24},{40,32},{48,40},{56,48},{9,1},{17,9},... | collective-permute-start | bytes 49160 | tf_op jit(solution)/shard_map/ppermute | solution.py:27
  228.1 7.9 %collective-permute-start.28 = (bf16[64,10,1]{2,1,0:T(8,128)(2,1)}, bf16[64,10,1]{2,1,0:T(8,128)(2,1)S(1)}, u32[]{:S(2)}, u32[]{:S(2)}) collective-permute-start(bf16[64,10,1]{2,1,0:T(8,128)(2,1)} %get-tuple-element.164), channel_id=1, source_target_pairs={{0,1},{1,2},{2,3},{3,4},{4,5},{5,6},{6,7},{8,9},{9,10},{10,11},{11... | collective-permute-start | bytes 3848 | tf_op jit(solution)/shard_map/ppermute | solution.py:25
  231.3 8.8 %collective-permute-start.29 = (bf16[64,10,1]{2,1,0:T(8,128)(2,1)}, bf16[64,10,1]{2,1,0:T(8,128)(2,1)S(1)}, u32[]{:S(2)}, u32[]{:S(2)}) collective-permute-start(bf16[64,10,1]{2,1,0:T(8,128)(2,1)} %get-tuple-element.163), channel_id=1, source_target_pairs={{1,0},{2,1},{3,2},{4,3},{5,4},{6,5},{7,6},{9,8},{10,9},{11,10},{12... | collective-permute-start | bytes 3848 | tf_op jit(solution)/shard_map/ppermute | solution.py:27
  242.1 4.5 collective-permute-start.30
  244.5 5.2 %collective-permute-start.31 = (bf16[64,1,128]{2,1,0:T(2,128)(2,1)S(1)}, bf16[64,1,128]{2,1,0:T(2,128)(2,1)S(1)}, u32[]{:S(2)}, u32[]{:S(2)}) collective-permute-start(bf16[64,1,128]{2,1,0:T(2,128)(2,1)S(1)} %get-tuple-element.210), channel_id=1, source_target_pairs={{8,0},{16,8},{24,16},{32,24},{40,32},{48,40},{56,48},{9,1},{17,9},... | collective-permute-start | bytes 49160 | tf_op jit(solution)/shard_map/ppermute | solution.py:27
  250.8 7.9 %collective-permute-start.32 = (bf16[64,10,1]{2,1,0:T(8,128)(2,1)}, bf16[64,10,1]{2,1,0:T(8,128)(2,1)}, u32[]{:S(2)}, u32[]{:S(2)}) collective-permute-start(bf16[64,10,1]{2,1,0:T(8,128)(2,1)} %get-tuple-element.162), channel_id=1, source_target_pairs={{0,1},{1,2},{2,3},{3,4},{4,5},{5,6},{6,7},{8,9},{9,10},{10,11},{11... | collective-permute-start | bytes 3848 | tf_op jit(solution)/shard_map/ppermute | solution.py:25
  255.5 8.7 %collective-permute-start.33 = (bf16[64,10,1]{2,1,0:T(8,128)(2,1)}, bf16[64,10,1]{2,1,0:T(8,128)(2,1)S(1)}, u32[]{:S(2)}, u32[]{:S(2)}) collective-permute-start(bf16[64,10,1]{2,1,0:T(8,128)(2,1)} %get-tuple-element.161), channel_id=1, source_target_pairs={{1,0},{2,1},{3,2},{4,3},{5,4},{6,5},{7,6},{9,8},{10,9},{11,10},{12... | collective-permute-start | bytes 3848 | tf_op jit(solution)/shard_map/ppermute | solution.py:27
  268.3 6.0 %collective-permute-start.34 = (bf16[64,1,128]{2,1,0:T(2,128)(2,1)}, bf16[64,1,128]{2,1,0:T(2,128)(2,1)S(1)}, u32[]{:S(2)}, u32[]{:S(2)}) collective-permute-start(bf16[64,1,128]{2,1,0:T(2,128)(2,1)} %get-tuple-element.207), channel_id=1, source_target_pairs={{0,8},{8,16},{16,24},{24,32},{32,40},{40,48},{48,56},{1,9},{9,17},... | collective-permute-start | bytes 49160 | tf_op jit(solution)/shard_map/ppermute | solution.py:25
  270.2 5.6 %collective-permute-start.35 = (bf16[64,1,128]{2,1,0:T(2,128)(2,1)}, bf16[64,1,128]{2,1,0:T(2,128)(2,1)}, u32[]{:S(2)}, u32[]{:S(2)}) collective-permute-start(bf16[64,1,128]{2,1,0:T(2,128)(2,1)} %get-tuple-element.208), channel_id=1, source_target_pairs={{8,0},{16,8},{24,16},{32,24},{40,32},{48,40},{56,48},{9,1},{17,9},... | collective-permute-start | bytes 49160 | tf_op jit(solution)/shard_map/ppermute | solution.py:27
  277.5 8.7 %collective-permute-start.36 = (bf16[64,10,1]{2,1,0:T(8,128)(2,1)}, bf16[64,10,1]{2,1,0:T(8,128)(2,1)}, u32[]{:S(2)}, u32[]{:S(2)}) collective-permute-start(bf16[64,10,1]{2,1,0:T(8,128)(2,1)} %get-tuple-element.160), channel_id=1, source_target_pairs={{0,1},{1,2},{2,3},{3,4},{4,5},{5,6},{6,7},{8,9},{9,10},{10,11},{11... | collective-permute-start | bytes 3848 | tf_op jit(solution)/shard_map/ppermute | solution.py:25
  285.0 9.3 %collective-permute-start.37 = (bf16[64,10,1]{2,1,0:T(8,128)(2,1)}, bf16[64,10,1]{2,1,0:T(8,128)(2,1)S(1)}, u32[]{:S(2)}, u32[]{:S(2)}) collective-permute-start(bf16[64,10,1]{2,1,0:T(8,128)(2,1)} %get-tuple-element.159), channel_id=1, source_target_pairs={{1,0},{2,1},{3,2},{4,3},{5,4},{6,5},{7,6},{9,8},{10,9},{11,10},{12... | collective-permute-start | bytes 3848 | tf_op jit(solution)/shard_map/ppermute | solution.py:27
  298.6 9.9 %collective-permute-start.38 = (bf16[64,1,128]{2,1,0:T(2,128)(2,1)}, bf16[64,1,128]{2,1,0:T(2,128)(2,1)S(1)}, u32[]{:S(2)}, u32[]{:S(2)}) collective-permute-start(bf16[64,1,128]{2,1,0:T(2,128)(2,1)} %get-tuple-element.205), channel_id=1, source_target_pairs={{0,8},{8,16},{16,24},{24,32},{32,40},{40,48},{48,56},{1,9},{9,17},... | collective-permute-start | bytes 49160 | tf_op jit(solution)/shard_map/ppermute | solution.py:25
  300.5 8.0 %collective-permute-start.39 = (bf16[64,1,128]{2,1,0:T(2,128)(2,1)}, bf16[64,1,128]{2,1,0:T(2,128)(2,1)S(1)}, u32[]{:S(2)}, u32[]{:S(2)}) collective-permute-start(bf16[64,1,128]{2,1,0:T(2,128)(2,1)} %get-tuple-element.206), channel_id=1, source_target_pairs={{8,0},{16,8},{24,16},{32,24},{40,32},{48,40},{56,48},{9,1},{17,9},... | collective-permute-start | bytes 49160 | tf_op jit(solution)/shard_map/ppermute | solution.py:27
  308.8 8.5 %collective-permute-start.40 = (bf16[64,10,1]{2,1,0:T(8,128)(2,1)S(1)}, bf16[64,10,1]{2,1,0:T(8,128)(2,1)S(1)}, u32[]{:S(2)}, u32[]{:S(2)}) collective-permute-start(bf16[64,10,1]{2,1,0:T(8,128)(2,1)S(1)} %get-tuple-element.158), channel_id=1, source_target_pairs={{0,1},{1,2},{2,3},{3,4},{4,5},{5,6},{6,7},{8,9},{9,10},{10,11},{11... | collective-permute-start | bytes 3848 | tf_op jit(solution)/shard_map/ppermute | solution.py:25
  311.8 9.9 %collective-permute-start.41 = (bf16[64,10,1]{2,1,0:T(8,128)(2,1)S(1)}, bf16[64,10,1]{2,1,0:T(8,128)(2,1)S(1)}, u32[]{:S(2)}, u32[]{:S(2)}) collective-permute-start(bf16[64,10,1]{2,1,0:T(8,128)(2,1)S(1)} %get-tuple-element.157), channel_id=1, source_target_pairs={{1,0},{2,1},{3,2},{4,3},{5,4},{6,5},{7,6},{9,8},{10,9},{11,10},{12... | collective-permute-start | bytes 3848 | tf_op jit(solution)/shard_map/ppermute | solution.py:27
  323.9 4.8 collective-permute-start.42
  325.8 5.2 %collective-permute-start.43 = (bf16[64,1,128]{2,1,0:T(2,128)(2,1)S(1)}, bf16[64,1,128]{2,1,0:T(2,128)(2,1)S(1)}, u32[]{:S(2)}, u32[]{:S(2)}) collective-permute-start(bf16[64,1,128]{2,1,0:T(2,128)(2,1)S(1)} %get-tuple-element.204), channel_id=1, source_target_pairs={{8,0},{16,8},{24,16},{32,24},{40,32},{48,40},{56,48},{9,1},{17,9},... | collective-permute-start | bytes 49160 | tf_op jit(solution)/shard_map/ppermute | solution.py:27
  331.4 7.9 %collective-permute-start.44 = (bf16[64,10,1]{2,1,0:T(8,128)(2,1)S(1)}, bf16[64,10,1]{2,1,0:T(8,128)(2,1)S(1)}, u32[]{:S(2)}, u32[]{:S(2)}) collective-permute-start(bf16[64,10,1]{2,1,0:T(8,128)(2,1)S(1)} %get-tuple-element.156), channel_id=1, source_target_pairs={{0,1},{1,2},{2,3},{3,4},{4,5},{5,6},{6,7},{8,9},{9,10},{10,11},{11... | collective-permute-start | bytes 3848 | tf_op jit(solution)/shard_map/ppermute | solution.py:25
  334.8 9.0 %collective-permute-start.45 = (bf16[64,10,1]{2,1,0:T(8,128)(2,1)S(1)}, bf16[64,10,1]{2,1,0:T(8,128)(2,1)S(1)}, u32[]{:S(2)}, u32[]{:S(2)}) collective-permute-start(bf16[64,10,1]{2,1,0:T(8,128)(2,1)S(1)} %get-tuple-element.155), channel_id=1, source_target_pairs={{1,0},{2,1},{3,2},{4,3},{5,4},{6,5},{7,6},{9,8},{10,9},{11,10},{12... | collective-permute-start | bytes 3848 | tf_op jit(solution)/shard_map/ppermute | solution.py:27
  346.0 4.8 collective-permute-start.46
  347.9 5.2 %collective-permute-start.47 = (bf16[64,1,128]{2,1,0:T(2,128)(2,1)S(1)}, bf16[64,1,128]{2,1,0:T(2,128)(2,1)S(1)}, u32[]{:S(2)}, u32[]{:S(2)}) collective-permute-start(bf16[64,1,128]{2,1,0:T(2,128)(2,1)S(1)} %get-tuple-element.202), channel_id=1, source_target_pairs={{8,0},{16,8},{24,16},{32,24},{40,32},{48,40},{56,48},{9,1},{17,9},... | collective-permute-start | bytes 49160 | tf_op jit(solution)/shard_map/ppermute | solution.py:27
  353.5 7.7 %collective-permute-start.48 = (bf16[64,10,1]{2,1,0:T(8,128)(2,1)S(1)}, bf16[64,10,1]{2,1,0:T(8,128)(2,1)S(1)}, u32[]{:S(2)}, u32[]{:S(2)}) collective-permute-start(bf16[64,10,1]{2,1,0:T(8,128)(2,1)S(1)} %get-tuple-element.154), channel_id=1, source_target_pairs={{0,1},{1,2},{2,3},{3,4},{4,5},{5,6},{6,7},{8,9},{9,10},{10,11},{11... | collective-permute-start | bytes 3848 | tf_op jit(solution)/shard_map/ppermute | solution.py:25
  357.1 153.6 %all-reduce.5.cloned.1.call-start = ((), (), s32[]{:S(2)}) async-start(), calls=%async_computation.1 | async-start | bytes 1310720 | tf_op jit(solution)/shard_map/psum | solution.py:11
  357.2 9.0 %collective-permute-start.49 = (bf16[64,10,1]{2,1,0:T(8,128)(2,1)S(1)}, bf16[64,10,1]{2,1,0:T(8,128)(2,1)S(1)}, u32[]{:S(2)}, u32[]{:S(2)}) collective-permute-start(bf16[64,10,1]{2,1,0:T(8,128)(2,1)S(1)} %get-tuple-element.153), channel_id=1, source_target_pairs={{1,0},{2,1},{3,2},{4,3},{5,4},{6,5},{7,6},{9,8},{10,9},{11,10},{12... | collective-permute-start | bytes 3848 | tf_op jit(solution)/shard_map/ppermute | solution.py:27
  435.0 7.1 %collective-permute-start.1 = (f32[64,1024]{1,0:T(8,128)S(1)}, f32[64,1024]{1,0:T(8,128)S(1)}, u32[]{:S(2)}, u32[]{:S(2)}) collective-permute-start(f32[64,1024]{1,0:T(8,128)S(1)} %convolution_add_fusion.5), channel_id=1, source_target_pairs={{64,0},{128,64},{192,128},{256,192},{320,256},{384,320},{448,384},... | collective-permute-start | bytes 786440 | tf_op jit(solution)/shard_map/while/body/eval_jaxpr/ppermute | solution.py:37
  442.5 8.1 %collective-permute-start.1 = (f32[64,1024]{1,0:T(8,128)S(1)}, f32[64,1024]{1,0:T(8,128)S(1)}, u32[]{:S(2)}, u32[]{:S(2)}) collective-permute-start(f32[64,1024]{1,0:T(8,128)S(1)} %convolution_add_fusion.5), channel_id=1, source_target_pairs={{64,0},{128,64},{192,128},{256,192},{320,256},{384,320},{448,384},... | collective-permute-start | bytes 786440 | tf_op jit(solution)/shard_map/while/body/eval_jaxpr/ppermute | solution.py:37
  450.9 9.6 %collective-permute-start.1 = (f32[64,1024]{1,0:T(8,128)S(1)}, f32[64,1024]{1,0:T(8,128)S(1)}, u32[]{:S(2)}, u32[]{:S(2)}) collective-permute-start(f32[64,1024]{1,0:T(8,128)S(1)} %convolution_add_fusion.5), channel_id=1, source_target_pairs={{64,0},{128,64},{192,128},{256,192},{320,256},{384,320},{448,384},... | collective-permute-start | bytes 786440 | tf_op jit(solution)/shard_map/while/body/eval_jaxpr/ppermute | solution.py:37
  460.9 10.2 %collective-permute-start.1 = (f32[64,1024]{1,0:T(8,128)S(1)}, f32[64,1024]{1,0:T(8,128)S(1)}, u32[]{:S(2)}, u32[]{:S(2)}) collective-permute-start(f32[64,1024]{1,0:T(8,128)S(1)} %convolution_add_fusion.5), channel_id=1, source_target_pairs={{64,0},{128,64},{192,128},{256,192},{320,256},{384,320},{448,384},... | collective-permute-start | bytes 786440 | tf_op jit(solution)/shard_map/while/body/eval_jaxpr/ppermute | solution.py:37
  471.4 9.3 %collective-permute-start.1 = (f32[64,1024]{1,0:T(8,128)S(1)}, f32[64,1024]{1,0:T(8,128)S(1)}, u32[]{:S(2)}, u32[]{:S(2)}) collective-permute-start(f32[64,1024]{1,0:T(8,128)S(1)} %convolution_add_fusion.5), channel_id=1, source_target_pairs={{64,0},{128,64},{192,128},{256,192},{320,256},{384,320},{448,384},... | collective-permute-start | bytes 786440 | tf_op jit(solution)/shard_map/while/body/eval_jaxpr/ppermute | solution.py:37
  481.1 9.3 %collective-permute-start.1 = (f32[64,1024]{1,0:T(8,128)S(1)}, f32[64,1024]{1,0:T(8,128)S(1)}, u32[]{:S(2)}, u32[]{:S(2)}) collective-permute-start(f32[64,1024]{1,0:T(8,128)S(1)} %convolution_add_fusion.5), channel_id=1, source_target_pairs={{64,0},{128,64},{192,128},{256,192},{320,256},{384,320},{448,384},... | collective-permute-start | bytes 786440 | tf_op jit(solution)/shard_map/while/body/eval_jaxpr/ppermute | solution.py:37
  490.7 11.4 %collective-permute-start.1 = (f32[64,1024]{1,0:T(8,128)S(1)}, f32[64,1024]{1,0:T(8,128)S(1)}, u32[]{:S(2)}, u32[]{:S(2)}) collective-permute-start(f32[64,1024]{1,0:T(8,128)S(1)} %convolution_add_fusion.5), channel_id=1, source_target_pairs={{64,0},{128,64},{192,128},{256,192},{320,256},{384,320},{448,384},... | collective-permute-start | bytes 786440 | tf_op jit(solution)/shard_map/while/body/eval_jaxpr/ppermute | solution.py:37
  (27 other events, 162.3 us)
Sparse Core Ops, SparseCore 0:
  357.3 77.2 all-reduce.2
  436.9 73.7 all-reduce.4
